TPU v7x, 512 devices: a whole 4x4x16 slice. The times are simulated.
512 devices in a mesh: table: 128 (over z, x, core), seq: 4 (over y).
Axes of the slice: x: 4, y: 4, z: 16, core: 2. Of those that a mesh axis runs over, the one named last changes fastest.
Arguments:
- embedding_table: bfloat16 [65536, 512], P('table'), may hold values from -6 to 6
- project_in: bfloat16 [512, 2048], replicated, may hold values from -0.25 to 0.25
- project_out: bfloat16 [512, 512], replicated, may hold values from -0.25 to 0.25
- row_owner: int32 [65536, 1], P(('table', 'seq')), may hold values from 0 to 127; in each aligned block of 128 rows (0 to 127, 128 to 255, ...) at most 2 rows name the same one
- row_offset: int32 [65536], P(('table', 'seq')), may hold values from 0 to 511
- user_lengths: int32 [128, 3], P('table'), may hold values from 1 to 256, 512 in all within a row
- upstream: bfloat16 [65536, 512], P(('table', 'seq')), may hold values from -6 to 6
Outputs:
- layer_out: bfloat16 [65536, 512], P(('table', 'seq'))
- table_grad: float32 [65536, 512], P('table')
Inputs may be any that keep to these rules, and one draw needn't show every extreme that they name: `row_owner`: in each aligned block of 128 rows (the rows of one device) no owner is named by more than 2 rows, a bound that some block reaches. `user_lengths`: each row sums to 512.
All inputs are finite; a program needn't handle non-finite values.
Results may differ from a plain program's by a relative error of at most 0.0064.
Values may be sent and summed in bfloat16 or wider, within the bound.
A program may use at most 64 MiB of HBM per device.

v0:
```python
import jax
import jax.numpy as jnp
from jax import lax
from jax.sharding import PartitionSpec as P

HEADS = 4


EPS = 1e-05


def silu_slope(inputs):
    logistic = jax.nn.sigmoid(inputs)
    return logistic * (1.0 + inputs * (1.0 - logistic))


def normalize(inputs):
    center = inputs - jnp.mean(inputs, axis=-1, keepdims=True)
    inv_scale = lax.rsqrt(jnp.mean(center * center, axis=-1, keepdims=True) + EPS)
    return (center * inv_scale, inv_scale)


def normalize_back(grad_in, normed, inv_scale):
    return inv_scale * (
        grad_in
        - jnp.mean(grad_in, axis=-1, keepdims=True)
        - normed * jnp.mean(grad_in * normed, axis=-1, keepdims=True)
    )


def allowed_pairs(query_index, key_index, bounds):
    query_user = jnp.sum((query_index[:, None] >= bounds[None, :]).astype(jnp.int32), axis=1)
    key_user = jnp.sum((key_index[:, None] >= bounds[None, :]).astype(jnp.int32), axis=1)
    same_user = (query_user[:, None] == key_user[None, :]) & (
        key_index[None, :] <= query_index[:, None]
    )
    return same_user.astype(jnp.float32)


def split_heads(matrix):
    return matrix.reshape(matrix.shape[0], HEADS, matrix.shape[1] // HEADS)


def pair_products(left_rows, right_rows):
    return jnp.einsum(
        "qhe,khe->hqk",
        split_heads(left_rows),
        split_heads(right_rows),
        preferred_element_type=jnp.float32,
    )


def spread_keys(weights, right_rows):
    summed = jnp.einsum(
        "hqk,khe->qhe", weights, split_heads(right_rows), preferred_element_type=jnp.float32
    )
    return summed.reshape(summed.shape[0], -1)


def spread_queries(weights, left_rows):
    summed = jnp.einsum(
        "hqk,qhe->khe", weights, split_heads(left_rows), preferred_element_type=jnp.float32
    )
    return summed.reshape(summed.shape[0], -1)


def local(embedding_table, project_in, project_out, row_owner, row_offset, user_lengths, upstream):
    tokens = row_offset.shape[0]
    width = project_out.shape[0]
    table_size = lax.axis_size("table")
    capacity = max(2, 2 * tokens // table_size)
    owner_index = row_owner[:, 0]
    chosen = (owner_index[:, None] == jnp.arange(table_size, dtype=jnp.int32)[None, :]).astype(
        jnp.int32
    )
    earlier = jnp.cumsum(chosen, axis=0) - chosen
    slot_index = jnp.sum(earlier * chosen, axis=1)
    flat_slot = owner_index * capacity + slot_index
    requests = jnp.zeros((table_size * capacity,), jnp.int32).at[flat_slot].set(row_offset)
    received = lax.all_to_all(
        requests.reshape(table_size, capacity), "table", split_axis=0, concat_axis=0, tiled=True
    )
    wanted = received.reshape(table_size * capacity)
    replies = jnp.take(embedding_table, wanted, axis=0).reshape(table_size, capacity, width)
    answered = lax.all_to_all(replies, "table", split_axis=0, concat_axis=0, tiled=True)
    embedded = jnp.take(answered.reshape(table_size * capacity, width), flat_slot, axis=0)
    normed, inv_scale = normalize(embedded.astype(jnp.float32))
    projected = jnp.dot(normed.astype(jnp.bfloat16), project_in, preferred_element_type=jnp.float32)
    activated = jax.nn.silu(projected).astype(jnp.bfloat16)
    gate_u = activated[:, :width]
    values = activated[:, width : 2 * width]
    queries = activated[:, 2 * width : 3 * width]
    keys = activated[:, 3 * width :]
    all_keys, all_values = (
        lax.all_gather(keys, "seq", axis=0, tiled=True),
        lax.all_gather(values, "seq", axis=0, tiled=True),
    )
    group_len = all_keys.shape[0]
    bounds = jnp.cumsum(user_lengths[0])
    query_index = lax.axis_index("seq") * tokens + jnp.arange(tokens, dtype=jnp.int32)
    key_index = jnp.arange(group_len, dtype=jnp.int32)
    allowed = allowed_pairs(query_index, key_index, bounds)[None]
    score_scale = (width // HEADS) ** (-0.5)
    scores = pair_products(queries, all_keys) * score_scale
    weights = (jax.nn.silu(scores) * allowed).astype(jnp.bfloat16)
    attended = spread_keys(weights, all_values)
    attn_normed, attn_inv = normalize(attended)
    gated = attn_normed * gate_u.astype(jnp.float32)
    residual_sum = embedded.astype(jnp.float32) + jnp.dot(
        gated.astype(jnp.bfloat16), project_out, preferred_element_type=jnp.float32
    )
    layer_out = residual_sum.astype(jnp.bfloat16)
    grad_gated = lax.dot_general(
        upstream, project_out, (((1,), (1,)), ((), ())), preferred_element_type=jnp.float32
    )
    grad_gate = grad_gated * attn_normed
    grad_out = normalize_back(
        grad_gated * gate_u.astype(jnp.float32), attn_normed, attn_inv
    ).astype(jnp.bfloat16)
    grad_attn = pair_products(grad_out, all_values)
    grad_score = (grad_attn * silu_slope(scores) * allowed * score_scale).astype(jnp.bfloat16)
    grad_query = spread_keys(grad_score, all_keys)
    shares = lax.psum_scatter(
        jnp.concatenate(
            [spread_queries(grad_score, queries), spread_queries(weights, grad_out)], axis=1
        ),
        "seq",
        scatter_dimension=0,
        tiled=True,
    )
    grad_key = shares[:, :width]
    grad_value = shares[:, width:]
    grad_acts = jnp.concatenate([grad_gate, grad_value, grad_query, grad_key], axis=1)
    grad_projected = (grad_acts * silu_slope(projected)).astype(jnp.bfloat16)
    grad_normed = lax.dot_general(
        grad_projected, project_in, (((1,), (1,)), ((), ())), preferred_element_type=jnp.float32
    )
    grad_embed = upstream.astype(jnp.float32) + normalize_back(grad_normed, normed, inv_scale)
    outgoing = jnp.zeros((table_size * capacity, width), jnp.float32).at[flat_slot].set(grad_embed)
    incoming = lax.all_to_all(
        outgoing.reshape(table_size, capacity, width),
        "table",
        split_axis=0,
        concat_axis=0,
        tiled=True,
    )
    partial_grad = (
        jnp.zeros((embedding_table.shape[0], width), jnp.float32)
        .at[wanted]
        .add(incoming.reshape(table_size * capacity, width))
    )
    table_grad = lax.psum(partial_grad, "seq")
    return (layer_out, table_grad)


def solution(mesh):
    return jax.shard_map(
        local,
        mesh=mesh,
        in_specs=(
            P("table", None),
            P(),
            P(),
            P(("table", "seq"), None),
            P(("table", "seq")),
            P("table", None),
            P(("table", "seq"), None),
        ),
        out_specs=(P(("table", "seq"), None), P("table", None)),
        check_vma=False,
    )
```

profile of v0, /device:TPU:1, one launch (start us, length us, event | category | flops | bytes accessed | tf_op | source)
XLA Modules:
  0.0 277.9 jit_solution(17265895367555920373)
XLA Ops:
  7.2 0.9 fusion.48
  8.3 0.8 select_reduce_fusion
  9.1 0.7 and_bitcast_fusion
  9.8 1.1 scatter_custom_fusion
  11.0 35.1 %all_to_all.19 = s32[128,1,2]{2,1,0:T(1,128)S(1)} all-to-all(s32[128,1,2]{2,1,0:T(1,128)S(1)} %bitcast.76), channel_id=1, replica_groups=mesh['table'=128,'seq'=4] {'table'}, dimensions={0} | all-to-all | bytes 2048 | tf_op jit(solution)/shard_map/all_to_all | solution.py:80
  46.2 0.5 broadcast.198
  46.7 0.8 reduce.6
  47.7 1.2 gather_fusion
  48.9 1.0 broadcast_select_fusion
  50.0 5.7 %all-to-all-start.1 = ((bf16[128,2,512]{2,1,0:T(2,128)(2,1)}), bf16[128,2,512]{2,1,0:T(2,128)(2,1)S(1)}, u32[]{:S(2)}, u32[]{:S(2)}) async-start(bf16[128,2,512]{2,1,0:T(2,128)(2,1)} %broadcast_select_fusion), calls=%async_computation.1 | async-start | bytes 524288 | tf_op jit(solution)/shard_map/all_to_all | solution.py:85
  56.1 0.8 fusion.33
  56.9 19.4 %all-to-all-done.1 = bf16[128,2,512]{2,1,0:T(2,128)(2,1)S(1)} async-done(((bf16[128,2,512]{2,1,0:T(2,128)(2,1)}), bf16[128,2,512]{2,1,0:T(2,128)(2,1)S(1)}, u32[]{:S(2)}, u32[]{:S(2)}) %all-to-all-start.1) | async-done | bytes 262176 | tf_op jit(solution)/shard_map/all_to_all | solution.py:85
  76.4 0.8 gather_fusion.1
  77.6 1.5 multiply_convert_fusion.1
  79.2 0.8 copy-done.10
  80.1 11.8 %all_gather.6 = bf16[512,512]{1,0:T(8,128)(2,1)} all-gather(bf16[128,512]{1,0:T(8,128)(2,1)S(1)} %get-tuple-element.12), channel_id=1, replica_groups=mesh['table'=128,'seq'=4] {'seq'}, dimensions={0}, use_global_device_ids=true | all-gather | bytes 655360 | tf_op jit(solution)/shard_map/all_gather | solution.py:96
  92.0 9.9 %all_gather.7 = bf16[512,512]{1,0:T(8,128)(2,1)S(1)} all-gather(bf16[128,512]{1,0:T(8,128)(2,1)S(1)} %get-tuple-element.13), channel_id=1, replica_groups=mesh['table'=128,'seq'=4] {'seq'}, dimensions={0}, use_global_device_ids=true | all-gather | bytes 655360 | tf_op jit(solution)/shard_map/all_gather | solution.py:95
  101.8 0.2 copy.64
  102.1 0.8 copy-done.6
  102.9 2.5 multiply_convert_fusion
  105.4 0.4 fusion.56
  105.9 0.3 copy-done.5
  106.4 0.3 copy-done.2
  106.7 1.3 fusion.47
  108.0 1.7 fusion.34
  109.7 0.8 copy.65
  110.5 1.4 fusion.58
  111.9 2.1 fusion.2
  114.0 0.8 copy-done.8
  114.8 1.3 fusion.57
  116.1 2.5 copy.60
  118.6 1.3 copy.61
  119.9 3.1 %pad_maximum_fusion = f32[512,1024]{1,0:T(8,128)} fusion(f32[512,512]{1,0:T(8,128)} %copy.61, f32[512,512]{1,0:T(8,128)} %copy.60), kind=kLoop, calls=%fused_computation.5 | loop fusion | flops 524288 | bytes 4194304 | tf_op jit(solution)/shard_map/concatenate | solution.py:124
  123.1 0.2 all-reduce.2.cloned.1.call-start
  123.3 0.8 copy-done.7
  124.3 1.0 fusion.59
  125.3 1.1 copy.62
  126.3 33.2 %reduce-scatter.2.cloned.1.call-done = f32[128,1024]{1,0:T(8,128)} async-done(((f32[512,1024]{1,0:T(8,128)}), f32[128,1024]{1,0:T(8,128)}) %reduce-scatter.2.cloned.1.call-update) | async-done | bytes 524304 | tf_op jit(solution)/shard_map/reduce_scatter | solution.py:123
  159.5 1.1 fusion.54
  160.6 2.2 fusion.53
  162.9 1.4 scatter_custom_fusion.1
  164.3 0.3 reshape.233
  164.7 47.4 %all_to_all.20 = f32[128,2,512]{2,1,0:T(2,128)} all-to-all(f32[128,2,512]{2,1,0:T(2,128)S(1)} %reshape.233), channel_id=1, replica_groups=mesh['table'=128,'seq'=4] {'table'}, dimensions={0} | all-to-all | bytes 1048576 | tf_op jit(solution)/shard_map/all_to_all | solution.py:140
  212.1 1.4 reshape.271
  213.5 3.1 %scatter_custom_fusion.2 = f32[512,512]{1,0:T(8,128)} fusion(s32[256]{0:T(256)S(1)} %bitcast.80, f32[256,512]{1,0:T(8,128)S(1)} %reshape.271, f32[]{:T(128)} %constant.68.clone.1), kind=kCustom, calls=%fused_computation.22 | custom fusion | flops 131072 | bytes 1048580 | tf_op jit(solution)/shard_map/scatter-add | solution.py:150
  216.6 1.8 fusion.3
  218.4 50.4 %all-reduce.2.cloned.1.call-done = f32[512,512]{1,0:T(8,128)} async-done(((f32[512,512]{1,0:T(8,128)}), f32[512,512]{1,0:T(8,128)}) %all-reduce.2.cloned.1.call-update) | async-done | bytes 1048592 | tf_op jit(solution)/shard_map/psum | solution.py:152
  268.8 2.3 copy.78
  (65 shorter events, 2.1 us)
Async XLA Ops:
  7.2 70.5 %copy-start = (bf16[512,2048]{1,0:T(8,128)(2,1)S(1)}, bf16[512,2048]{1,0:T(8,128)(2,1)}, u32[]{:S(2)}) copy-start(bf16[512,2048]{1,0:T(8,128)(2,1)} %param.8) | copy-start | bytes 6291460
  7.2 40.5 %copy-start.1 = (bf16[512,512]{1,0:T(8,128)(2,1)S(1)}, bf16[512,512]{1,0:T(8,128)(2,1)}, u32[]{:S(2)}) copy-start(bf16[512,512]{1,0:T(8,128)(2,1)} %param.7) | copy-start | bytes 1572868
  9.8 46.1 %copy-start.17 = (s32[128,1]{0,1:T(1,128)}, s32[128,1]{0,1:T(1,128)S(1)}, u32[]{:S(2)}) copy-start(s32[128,1]{0,1:T(1,128)S(1)} %get-tuple-element.7) | copy-start | bytes 1540
  46.1 9.6 %copy-start.20 = (s32[1,3]{1,0:T(1,128)S(1)}, s32[1,3]{1,0:T(1,128)}, u32[]{:S(2)}) copy-start(s32[1,3]{1,0:T(1,128)} %param.12) | copy-start | bytes 40
  50.0 26.3 %all-to-all-start.1 = ((bf16[128,2,512]{2,1,0:T(2,128)(2,1)}), bf16[128,2,512]{2,1,0:T(2,128)(2,1)S(1)}, u32[]{:S(2)}, u32[]{:S(2)}) async-start(bf16[128,2,512]{2,1,0:T(2,128)(2,1)} %broadcast_select_fusion), calls=%async_computation.1 | async-start | bytes 524288 | tf_op jit(solution)/shard_map/all_to_all | solution.py:85
  55.6 103.9 %reduce-scatter.2.cloned.1.call-start = ((), (), s32[]{:S(2)}) async-start(), calls=%async_computation.4 | async-start | bytes 2621440 | tf_op jit(solution)/shard_map/reduce_scatter | solution.py:123
  77.4 1.8 copy-start.15
  77.6 1.5 copy-start.18
  79.2 0.8 copy-start.10
  80.1 22.0 %copy-start.13 = (bf16[128,512]{0,1:T(8,128)(2,1)}, bf16[128,512]{0,1:T(8,128)(2,1)S(1)}, u32[]{:S(2)}) copy-start(bf16[128,512]{0,1:T(8,128)(2,1)S(1)} %copy.63) | copy-start | bytes 393220
  102.1 0.8 copy-start.6
  102.9 2.6 copy-start.4
  105.4 0.8 copy-start.5
  105.4 1.2 copy-start.2
  105.4 1.2 copy-start.11
  111.9 2.9 %copy-start.14 = (bf16[128,512]{0,1:T(8,128)(2,1)S(1)}, bf16[128,512]{0,1:T(8,128)(2,1)}, u32[]{:S(2)}) copy-start(bf16[128,512]{0,1:T(8,128)(2,1)} %copy-done.13) | copy-start | bytes 393220
  114.0 0.8 copy-start.8
  123.1 1.0 copy-start.7
  123.1 1.2 copy-start.9
  123.1 145.7 %all-reduce.2.cloned.1.call-start = ((), (), s32[]{:S(2)}) async-start(), calls=%async_computation.5 | async-start | bytes 2097152 | tf_op jit(solution)/shard_map/psum | solution.py:152
  160.6 2.3 copy-start.12
  160.6 2.3 copy-start.16
  160.6 2.3 copy-start.19
  164.6 51.9 %copy-start.3 = (bf16[512,512]{1,0:T(8,128)(2,1)S(1)}, bf16[512,512]{1,0:T(8,128)(2,1)}, u32[]{:S(2)}) copy-start(bf16[512,512]{1,0:T(8,128)(2,1)} %param.9) | copy-start | bytes 1572868
Sparse Core Ops, SparseCore 0:
  123.2 36.2 reduce-scatter.1
  216.7 52.0 all-reduce.1
where the time goes:
time: 279 us; the launch traced here: 278 us
  blocking collectives  104 us (37%)
  waiting for transfers between devices  103 us (37%)
  local copies, waits for them, and re-layouts  19.3 us (7%)
  matrix products  15.6 us (6%)
  other arithmetic  15.5 us (6%)
  between operations  14.4 us (5%)
  starting transfers between devices  5.94 us (2%)
    psum x1, waiting for transfers between devices, local(): table_grad = lax.psum(partial_grad, 'seq')  50.4 us
    all_to_all x1, blocking collectives, local(): lax.all_to_all(outgoing.reshape(table_size, capacity, width), 'table', sp...  47.4 us
    all_to_all x1, blocking collectives, local(): lax.all_to_all(requests.reshape(table_size, capacity), 'table', split_axi...  35.1 us
    reduce_scatter x1, waiting for transfers between devices, local(): lax.psum_scatter(jnp.concatenate([spread_queries(grad_score, queries), sp...  33.2 us
    all_to_all x1, waiting for transfers between devices, local(): lax.all_to_all(replies, 'table', split_axis=0, concat_axis=0, tiled=True)  19.4 us
    all_gather x1, blocking collectives, local(): lax.all_gather(values, 'seq', axis=0, tiled=True)  11.8 us
    all_gather x1, blocking collectives, local(): lax.all_gather(keys, 'seq', axis=0, tiled=True)  9.89 us
    unnamed x43, local copies, waits for them, and re-layouts  6.29 us
  transfers between devices with their start and end apart: 3, of which 3 were waited for; matrix products, arithmetic and copies ran while one was open for 2% of the time, Pallas kernels for 0%

commit v1 on v0

v1 whole, which is shorter than its diff:
```python
import functools

import jax
import jax.numpy as jnp
from jax import lax
from jax.experimental import pallas as pl
from jax.experimental.pallas import tpu as pltpu
from jax.sharding import PartitionSpec as P

HEADS = 4
EPS = 1e-05
PEERS = 8
PARTS = 2
F32 = jnp.float32
BF16 = jnp.bfloat16


def mul_nn(left, right):
    return lax.dot_general(left, right, (((1,), (0,)), ((), ())), preferred_element_type=F32)


def mul_nt(left, right):
    return lax.dot_general(left, right, (((1,), (1,)), ((), ())), preferred_element_type=F32)


def iota(shape, axis):
    return lax.broadcasted_iota(jnp.int32, shape, axis)


def kernel(
    ring,
    owner_ref,
    offset_ref,
    lengths_ref,
    table_hbm,
    w_in_hbm,
    w_out_hbm,
    up_hbm,
    layer_hbm,
    grad_hbm,
    id_near,
    id_all,
    slot_rows,
    table,
    w_in,
    w_out,
    up_all,
    w_head,
    rows_out,
    rows_z,
    rows_x,
    rows_in,
    emb_all,
    normed_bf,
    pre,
    act,
    kv_rows,
    weights,
    slopes,
    grad_gated,
    attended,
    sums,
    gated_out,
    gated_in,
    gp_out,
    gp_in,
    normed_t,
    up_t,
    g_out,
    g_z,
    g_x,
    g_in,
    layer_v,
    grad_v,
    local_sem,
    send_sem,
    recv_sem,
):
    tokens = 128
    width = table.shape[1]
    head = width // HEADS
    part = width // PARTS
    slots = 2 * PEERS * ring
    block = 2 * PEERS
    chunk_rows = 2 * ring
    me = lax.axis_index("table")
    seq = lax.axis_index("seq")
    z = me // PEERS
    p = me % PEERS

    def near(step):
        return (z * PEERS + (p + step) % PEERS, seq)

    def far(step):
        return (((z + step) % ring) * PEERS + p, seq)

    def beside(step):
        return (me, (seq + step) % HEADS)

    def send(src, dst, group, device):
        pltpu.make_async_remote_copy(
            src_ref=src,
            dst_ref=dst,
            send_sem=send_sem.at[group],
            recv_sem=recv_sem.at[group],
            device_id=device,
            device_id_type=pl.DeviceIdType.MESH,
        ).start()

    def await_bytes(view, sem):
        pltpu.make_async_copy(view, view, sem).wait()

    def rows(start, size):
        return pl.ds(pl.multiple_of(start, size), size)

    ID_NEAR, ID_FAR, UP, SLOTS, SUMS, GATED = range(6)
    GP = 6
    Z0 = 10
    X0 = Z0 + PARTS
    Y0 = X0 + PARTS
    GZ0 = Y0 + PARTS
    GX0 = GZ0 + PARTS
    GY0 = GX0 + PARTS

    up_copy = pltpu.make_async_copy(up_hbm, up_all.at[rows(seq * tokens, tokens), :], local_sem.at[0])
    up_copy.start()
    table_copy = pltpu.make_async_copy(table_hbm, table, local_sem.at[1])
    table_copy.start()
    in_copy = pltpu.make_async_copy(w_in_hbm, w_in, local_sem.at[2])
    in_copy.start()
    out_copy = pltpu.make_async_copy(w_out_hbm, w_out, local_sem.at[3])
    out_copy.start()

    owner = owner_ref[...]
    code = owner * table.shape[0] + offset_ref[...]
    id_near[p] = jnp.broadcast_to(code, (8, tokens))

    barrier = pltpu.get_barrier_semaphore()
    for step in range(1, PEERS):
        pl.semaphore_signal(barrier, inc=1, device_id=near(step), device_id_type=pl.DeviceIdType.MESH)
    for step in range(1, HEADS):
        pl.semaphore_signal(barrier, inc=1, device_id=beside(step), device_id_type=pl.DeviceIdType.MESH)

    @pl.loop(1, ring)
    def _(step):
        pl.semaphore_signal(barrier, inc=1, device_id=far(step), device_id_type=pl.DeviceIdType.MESH)

    pl.semaphore_wait(barrier, PEERS + ring + HEADS - 3)

    for step in range(1, PEERS):
        send(id_near.at[p], id_near.at[p], ID_NEAR, near(step))
    up_copy.wait()
    for step in range(1, HEADS):
        mine = up_all.at[rows(seq * tokens, tokens), :]
        send(mine, mine, UP, beside(step))

    owner_lane = jnp.broadcast_to(owner.astype(F32), (tokens, tokens))
    owner_sub = owner_lane.T
    n_sub = iota((tokens, tokens), 0)
    n_lane = iota((tokens, tokens), 1)
    same = owner_lane == owner_sub
    second_lane = jnp.max(jnp.where(same & (n_sub < n_lane), 1.0, 0.0), axis=0, keepdims=True)
    second_sub = jnp.max(jnp.where(same & (n_lane < n_sub), 1.0, 0.0), axis=1, keepdims=True)
    own_lane = owner
    slot_lane = (own_lane // PEERS) * block + second_lane.astype(jnp.int32) * PEERS + own_lane % PEERS
    own_sub = owner_sub[:, :1].astype(jnp.int32)
    slot_sub = (own_sub % PEERS) * chunk_rows + (own_sub // PEERS) * 2 + second_sub.astype(jnp.int32)
    pick_in = jnp.where(iota((tokens, slots), 1) == slot_sub, 1.0, 0.0).astype(BF16)
    place_out = jnp.where(iota((slots, tokens), 0) == slot_lane, 1.0, 0.0).astype(BF16)
    row_to = iota((slots, slots), 0)
    row_from = iota((slots, slots), 1)
    rest = row_to % chunk_rows
    source_row = (rest // 2) * block + (rest % 2) * PEERS + row_to // chunk_rows
    regroup = jnp.where(row_from == source_row, 1.0, 0.0).astype(BF16)

    await_bytes(id_near.at[pl.ds(0, PEERS - 1)], recv_sem.at[ID_NEAR])
    id_all[z] = jnp.concatenate([id_near[i, 0:1, :] for i in range(PEERS)], axis=0)

    @pl.loop(1, ring)
    def _(step):
        send(id_all.at[z], id_all.at[z], ID_FAR, far(step))

    in_copy.wait()
    for i in range(4):
        columns = pl.ds(pl.multiple_of(i * width + seq * head, head), head)
        w_head[i * head : (i + 1) * head, :] = w_in[:, columns].T
    table_copy.wait()
    out_copy.wait()

    await_bytes(id_all.at[pl.ds(0, ring - 1)], recv_sem.at[ID_FAR])
    codes = id_all[...].reshape(ring * PEERS, tokens)
    wanted = (codes // table.shape[0]) == me
    offsets = (codes % table.shape[0]).astype(F32)
    place = iota((ring * PEERS, tokens), 1).astype(F32)
    first = jnp.min(jnp.where(wanted, place, 1000.0), axis=1, keepdims=True)
    last = jnp.max(jnp.where(wanted, place, -1.0), axis=1, keepdims=True)
    first_off = jnp.sum(jnp.where(place == first, offsets, 0.0), axis=1, keepdims=True)
    last_off = jnp.sum(jnp.where(place == last, offsets, 0.0), axis=1, keepdims=True)
    none = float(table.shape[0])
    first_off = jnp.where(first < 1000.0, first_off, none)
    last_off = jnp.where(last > first, last_off, none)
    row_id = iota((ring * PEERS, table.shape[0]), 1).astype(F32)

    def interleave(one, two):
        both = [x.reshape(ring, PEERS, x.shape[1]) for x in (one, two)]
        return jnp.concatenate(both, axis=1).reshape(slots, one.shape[1])

    chosen = interleave(
        jnp.where(row_id == first_off, 1.0, 0.0), jnp.where(row_id == last_off, 1.0, 0.0)
    ).astype(BF16)
    for c in range(PARTS):
        rows_out[c] = mul_nn(chosen, table[:, c * part : (c + 1) * part]).astype(BF16)
        mine = rows(z * block, block)

        @pl.loop(1, ring)
        def _(step, c=c, mine=mine):
            there = rows(((z + step) % ring) * block, block)
            send(rows_out.at[c, there, :], rows_z.at[c, mine, :], Z0 + c, far(step))

        rows_z[c, mine, :] = rows_out[c, mine, :]

    slot_off = interleave(
        jnp.broadcast_to(first_off, (ring * PEERS, tokens)),
        jnp.broadcast_to(last_off, (ring * PEERS, tokens)),
    ).T[:8]
    high = jnp.floor(slot_off * 0.0625)
    digits = jnp.concatenate([high, slot_off - 16.0 * high], axis=0).astype(BF16)
    moved = mul_nt(digits, regroup)
    slot_rows[seq] = moved[:8] * 16.0 + moved[8:]
    for step in range(1, HEADS):
        send(slot_rows.at[seq], slot_rows.at[seq], SLOTS, beside(step))

    await_bytes(up_all.at[pl.ds(0, 3 * tokens), :], recv_sem.at[UP])
    grad_gated[...] = mul_nt(w_out[rows(seq * head, head), :], up_all[...])
    up_t[...] = up_all[rows(seq * tokens, tokens), :].astype(F32).T

    def pass_near(c, src, src_sem, mid, dst, base, sem):
        await_bytes(src.at[c, pl.ds(0, slots - block), :], recv_sem.at[src_sem + c])
        mid[c] = mul_nn(regroup, src[c]).astype(BF16)
        mine = rows(base + p * chunk_rows, chunk_rows)
        for step in range(1, PEERS):
            there = rows(((p + step) % PEERS) * chunk_rows, chunk_rows)
            send(mid.at[c, there, :], dst.at[c, mine, :], sem + c, near(step))
        dst[c, mine, :] = mid[c, rows(p * chunk_rows, chunk_rows), :]

    def gather_rows(c):
        await_bytes(rows_in.at[c, pl.ds(0, slots - chunk_rows), :], recv_sem.at[X0 + c])
        mine = rows(seq * tokens, tokens)
        emb_all[c, mine, :] = mul_nn(pick_in, rows_in[c]).astype(BF16)
        for step in range(1, HEADS):
            send(emb_all.at[c, mine, :], emb_all.at[c, mine, :], Y0 + c, beside(step))

    for c in range(PARTS):
        pass_near(c, rows_z, Z0, rows_x, rows_in, 0, X0)
        if c > 0:
            gather_rows(c - 1)
    gather_rows(PARTS - 1)

    own = rows(seq * tokens, tokens)
    emb_own = jnp.concatenate([emb_all[c, own, :] for c in range(PARTS)], axis=1).astype(F32)
    emb_t = emb_own.T
    centered_t = emb_t - jnp.mean(emb_t, axis=0, keepdims=True)
    inv_own = lax.rsqrt(jnp.mean(centered_t * centered_t, axis=0, keepdims=True) + EPS)
    normed_t[...] = centered_t * inv_own

    for c in range(PARTS):
        await_bytes(emb_all.at[c, pl.ds(0, 3 * tokens), :], recv_sem.at[Y0 + c])
    for i in range(HEADS):
        here = slice(i * tokens, (i + 1) * tokens)
        wide = jnp.concatenate([emb_all[c, here, :] for c in range(PARTS)], axis=1).astype(F32)
        centered = wide - jnp.mean(wide, axis=1, keepdims=True)
        inv = lax.rsqrt(jnp.mean(centered * centered, axis=1, keepdims=True) + EPS)
        normed_bf[here, :] = (centered * inv).astype(BF16)

    pre[...] = mul_nt(w_head[...], normed_bf[...])
    for i in range(4):
        here = slice(i * head, (i + 1) * head)
        x = pre[here, :]
        act[here, :] = (x * jax.nn.sigmoid(x)).astype(BF16)
    gate = slice(0, head)
    value = slice(head, 2 * head)
    query = slice(2 * head, 3 * head)
    key = slice(3 * head, 4 * head)
    kv_rows[0] = act[value, :].T
    kv_rows[1] = act[key, :].T

    start_two = lengths_ref[0, 0]
    start_three = start_two + lengths_ref[0, 1]

    def user_of(position):
        return (position >= start_two).astype(jnp.int32) + (position >= start_three).astype(jnp.int32)

    scale = head ** (-0.5)
    blocks = [slice(i * tokens, (i + 1) * tokens) for i in range(HEADS)]

    def keys_of(j):
        return slice(max(0, j - 2) * tokens, (j + 1) * tokens)

    def queries_of(i):
        return slice(i * tokens, min(HEADS, i + 3) * tokens)

    for j in range(HEADS):
        here, ms = blocks[j], keys_of(j)
        count = ms.stop - ms.start
        scores = mul_nn(kv_rows[1, ms, :], act[query, here]) * scale
        m_at = iota((count, 1), 0) + ms.start
        n_at = iota((1, tokens), 1) + here.start
        allowed = (user_of(m_at) == user_of(n_at)) & (m_at <= n_at)
        logistic = jax.nn.sigmoid(scores)
        weight = jnp.where(allowed, scores * logistic, 0.0).astype(BF16)
        weights[ms, here] = weight
        slopes[ms, here] = jnp.where(
            allowed, logistic * (1.0 + scores * (1.0 - logistic)) * scale, 0.0
        )
        out = mul_nn(act[value, ms], weight)
        attended[:, here] = out
        g = grad_gated[:, here] * act[gate, here].astype(F32)
        out_mean = jnp.mean(out, axis=0, keepdims=True)
        g_mean = jnp.mean(g, axis=0, keepdims=True)
        out_c = out - out_mean
        out_sq = jnp.sum(out_c * out_c, axis=0, keepdims=True)
        cross = jnp.sum(out_c * (g - g_mean), axis=0, keepdims=True)
        sums[seq, :, here] = jnp.concatenate(
            [out_mean, out_sq, g_mean, cross, jnp.zeros((4, tokens), F32)], axis=0
        )
    for step in range(1, HEADS):
        send(sums.at[seq], sums.at[seq], SUMS, beside(step))

    await_bytes(sums.at[pl.ds(0, HEADS - 1)], recv_sem.at[SUMS])
    parts = [sums[i] for i in range(HEADS)]
    means = [s[0:1] for s in parts]
    g_means = [s[2:3] for s in parts]
    out_mean = sum(means) * (1.0 / HEADS)
    g_mean = sum(g_means) * (1.0 / HEADS)
    out_sq = sum(s[1:2] for s in parts) + head * sum((m - out_mean) * (m - out_mean) for m in means)
    cross = sum(s[3:4] for s in parts) + head * sum(
        (m - out_mean) * (g - g_mean) for m, g in zip(means, g_means)
    )
    inv_out = lax.rsqrt(out_sq * (1.0 / width) + EPS)
    slant = inv_out * cross * (1.0 / width)

    def pre_slope(part_of, here):
        x = pre[part_of, here]
        logistic = jax.nn.sigmoid(x)
        return logistic * (1.0 + x * (1.0 - logistic))

    def exchange(i):
        here = pl.ds(i * head, head)
        mine = pl.ds(pl.multiple_of(i * width + seq * head, head), head)
        for step in range(1, HEADS):
            there = (seq + step) % HEADS
            send(gp_out.at[there, here, :], gp_in.at[mine, :], GP + i, beside(step))
        gp_in[mine, :] = gp_out[seq, here, :]

    grad_out = []
    for j in range(HEADS):
        here = blocks[j]
        gate_u = act[gate, here].astype(F32)
        raw = grad_gated[:, here]
        normed = (attended[:, here] - out_mean[:, here]) * inv_out[:, here]
        gated_out[j] = (normed * gate_u).astype(BF16)
        gp_out[j, gate, :] = (raw * normed * pre_slope(gate, here)).astype(BF16)
        grad_out.append(
            (
                inv_out[:, here]
                * (raw * gate_u - g_mean[:, here] - normed * slant[:, here])
            ).astype(BF16)
        )
    exchange(0)
    mine = rows(seq * head, head)
    for step in range(1, HEADS):
        send(gated_out.at[(seq + step) % HEADS], gated_in.at[mine, :], GATED, beside(step))
    gated_in[mine, :] = gated_out[seq]
    grad_out = jnp.concatenate(grad_out, axis=1)
    for i in range(HEADS):
        ns = queries_of(i)
        found = mul_nt(grad_out[:, ns], weights[blocks[i], ns])
        gp_out[i, value, :] = (found * pre_slope(value, blocks[i])).astype(BF16)
    exchange(1)
    grad_score = {}
    for j in range(HEADS):
        ms = keys_of(j)
        moved = mul_nn(kv_rows[0, ms, :], grad_out[:, blocks[j]])
        moved = (moved * slopes[ms, blocks[j]]).astype(BF16)
        grad_score[j] = moved
        weights[ms, blocks[j]] = moved
        found = mul_nn(act[key, ms], moved)
        gp_out[j, query, :] = (found * pre_slope(query, blocks[j])).astype(BF16)
    exchange(2)
    for i in range(HEADS):
        ns = queries_of(i)
        found = mul_nt(act[query, ns], weights[blocks[i], ns])
        gp_out[i, key, :] = (found * pre_slope(key, blocks[i])).astype(BF16)
    exchange(3)

    grad_normed = jnp.zeros((width, tokens), F32)
    for i in range(4):
        await_bytes(gp_in.at[pl.ds(i * width, 3 * head), :], recv_sem.at[GP + i])
        here = slice(i * width, (i + 1) * width)
        grad_normed = grad_normed + mul_nn(w_in[:, here], gp_in[here, :])
    normed = normed_t[...]
    grad_rows = up_t[...] + inv_own * (
        grad_normed
        - jnp.mean(grad_normed, axis=0, keepdims=True)
        - normed * jnp.mean(grad_normed * normed, axis=0, keepdims=True)
    )
    grad_rows = grad_rows.astype(BF16)
    for c in range(PARTS):
        g_out[c] = mul_nt(place_out, grad_rows[c * part : (c + 1) * part]).astype(BF16)
        mine = rows(z * block, block)

        @pl.loop(1, ring)
        def _(step, c=c, mine=mine):
            there = rows(((z + step) % ring) * block, block)
            send(g_out.at[c, there, :], g_z.at[c, mine, :], GZ0 + c, far(step))

        g_z[c, mine, :] = g_out[c, mine, :]

    await_bytes(gated_in.at[pl.ds(0, 3 * head), :], recv_sem.at[GATED])
    layer_v[...] = (emb_own + mul_nn(gated_in[...].T, w_out[...])).astype(BF16)
    layer_copy = pltpu.make_async_copy(layer_v, layer_hbm, local_sem.at[4])
    layer_copy.start()

    await_bytes(slot_rows.at[pl.ds(0, HEADS - 1)], recv_sem.at[SLOTS])
    table_row = iota((table.shape[0], slots), 0).astype(F32)
    spread = jnp.concatenate(
        [
            jnp.where(table_row == slot_rows[i, 0:1, :], 1.0, 0.0).astype(BF16)
            for i in range(HEADS)
        ],
        axis=1,
    )

    def pass_beside(c):
        mine = rows(seq * slots, slots)
        await_bytes(g_in.at[c, pl.ds(0, slots - chunk_rows), :], recv_sem.at[GX0 + c])
        for step in range(1, HEADS):
            send(g_in.at[c, mine, :], g_in.at[c, mine, :], GY0 + c, beside(step))

    for c in range(PARTS):
        pass_near(c, g_z, GZ0, g_x, g_in, seq * slots, GX0)
        if c > 0:
            pass_beside(c - 1)
    pass_beside(PARTS - 1)
    grad_copies = []
    for c in range(PARTS):
        await_bytes(g_in.at[c, pl.ds(0, 3 * slots), :], recv_sem.at[GY0 + c])
        grad_v[c] = mul_nn(spread, g_in[c])
        copy = pltpu.make_async_copy(
            grad_v.at[c], grad_hbm.at[:, pl.ds(c * part, part)], local_sem.at[5 + c]
        )
        copy.start()
        grad_copies.append(copy)

    await_bytes(id_near.at[pl.ds(0, PEERS - 1)], send_sem.at[ID_NEAR])
    await_bytes(id_all.at[pl.ds(0, ring - 1)], send_sem.at[ID_FAR])
    await_bytes(up_all.at[pl.ds(0, 3 * tokens), :], send_sem.at[UP])
    await_bytes(slot_rows.at[pl.ds(0, HEADS - 1)], send_sem.at[SLOTS])
    await_bytes(sums.at[pl.ds(0, HEADS - 1)], send_sem.at[SUMS])
    await_bytes(gated_in.at[pl.ds(0, 3 * head), :], send_sem.at[GATED])
    for i in range(4):
        await_bytes(gp_in.at[pl.ds(i * width, 3 * head), :], send_sem.at[GP + i])
    for c in range(PARTS):
        await_bytes(rows_z.at[c, pl.ds(0, slots - block), :], send_sem.at[Z0 + c])
        await_bytes(rows_in.at[c, pl.ds(0, slots - chunk_rows), :], send_sem.at[X0 + c])
        await_bytes(emb_all.at[c, pl.ds(0, 3 * tokens), :], send_sem.at[Y0 + c])
        await_bytes(g_z.at[c, pl.ds(0, slots - block), :], send_sem.at[GZ0 + c])
        await_bytes(g_in.at[c, pl.ds(0, slots - chunk_rows), :], send_sem.at[GX0 + c])
        await_bytes(g_in.at[c, pl.ds(0, 3 * slots), :], send_sem.at[GY0 + c])
    layer_copy.wait()
    for copy in grad_copies:
        copy.wait()


def local(embedding_table, project_in, project_out, row_owner, row_offset, user_lengths, upstream):
    tokens = row_offset.shape[0]
    table_rows, width = embedding_table.shape
    ring = lax.axis_size("table") // PEERS
    group = tokens * HEADS
    slots = 2 * PEERS * ring
    part = width // PARTS
    head = width // HEADS
    any_spec = pl.BlockSpec(memory_space=pl.ANY)
    vmem_spec = pl.BlockSpec(memory_space=pltpu.VMEM)
    smem_spec = pl.BlockSpec(memory_space=pltpu.SMEM)
    vmem = pltpu.VMEM
    return pl.pallas_call(
        functools.partial(kernel, ring),
        out_shape=(
            jax.ShapeDtypeStruct((tokens, width), BF16),
            jax.ShapeDtypeStruct((table_rows, width), F32),
        ),
        in_specs=[vmem_spec, vmem_spec, smem_spec] + [any_spec] * 4,
        out_specs=(any_spec, any_spec),
        scratch_shapes=[
            vmem((PEERS, 8, tokens), jnp.int32),
            vmem((ring, PEERS, tokens), jnp.int32),
            vmem((HEADS, 8, slots), F32),
            vmem((table_rows, width), BF16),
            vmem((width, 4 * width), BF16),
            vmem((width, width), BF16),
            vmem((group, width), BF16),
            vmem((4 * head, width), BF16),
            vmem((PARTS, slots, part), BF16),
            vmem((PARTS, slots, part), BF16),
            vmem((PARTS, slots, part), BF16),
            vmem((PARTS, slots, part), BF16),
            vmem((PARTS, group, part), BF16),
            vmem((group, width), BF16),
            vmem((4 * head, group), F32),
            vmem((4 * head, group), BF16),
            vmem((2, group, head), BF16),
            vmem((group, group), BF16),
            vmem((group, group), F32),
            vmem((head, group), F32),
            vmem((head, group), F32),
            vmem((HEADS, 8, group), F32),
            vmem((HEADS, head, tokens), BF16),
            vmem((width, tokens), BF16),
            vmem((HEADS, 4 * head, tokens), BF16),
            vmem((4 * width, tokens), BF16),
            vmem((width, tokens), F32),
            vmem((width, tokens), F32),
            vmem((PARTS, slots, part), BF16),
            vmem((PARTS, slots, part), BF16),
            vmem((PARTS, slots, part), BF16),
            vmem((PARTS, HEADS * slots, part), BF16),
            vmem((tokens, width), BF16),
            vmem((PARTS, table_rows, part), F32),
            pltpu.SemaphoreType.DMA((5 + PARTS,)),
            pltpu.SemaphoreType.DMA((10 + 6 * PARTS,)),
            pltpu.SemaphoreType.DMA((10 + 6 * PARTS,)),
        ],
        compiler_params=pltpu.CompilerParams(
            collective_id=0, has_side_effects=True, vmem_limit_bytes=48 * 2**20
        ),
        name="hstu_step",
    )(
        row_owner.reshape(1, tokens),
        row_offset.reshape(1, tokens),
        user_lengths,
        embedding_table,
        project_in,
        project_out,
        upstream,
    )


def solution(mesh):
    return jax.shard_map(
        local,
        mesh=mesh,
        in_specs=(
            P("table", None),
            P(),
            P(),
            P(("table", "seq"), None),
            P(("table", "seq")),
            P("table", None),
            P(("table", "seq"), None),
        ),
        out_specs=(P(("table", "seq"), None), P("table", None)),
        check_vma=False,
    )
```

time: 279 us -> 110 us (0.39)
  blocking collectives: 104 us -> 0 us
  waiting for transfers between devices: 103 us -> 0 us
  Pallas kernels: 0 us -> 100 us
  matrix products: 15.6 us -> 0 us
  other arithmetic: 15.5 us -> 0 us
  between operations: 14.4 us -> 0.66 us
  local copies, waits for them, and re-layouts: 19.3 us -> 8.16 us
  starting transfers between devices: 5.94 us -> 0 us
    pallas_call x0 -> x1, Pallas kernels: none -> 100 us  [local(): pl.pallas_call(functools.partial(kernel, ring), out_shape=(jax.ShapeDtype...]
    all_to_all x2 -> x0, blocking collectives: 82.5 us -> none  [the longest x1 47.4 us: local(): lax.all_to_all(outgoing.reshape(table_size, capacity, width), 'table', sp...]
    psum x1 -> x0, waiting for transfers between devices: 50.4 us -> none  [local(): table_grad = lax.psum(partial_grad, 'seq')]
    reduce_scatter x1 -> x0, waiting for transfers between devices: 33.2 us -> none  [local(): lax.psum_scatter(jnp.concatenate([spread_queries(grad_score, queries), sp...]
    all_gather x2 -> x0, blocking collectives: 21.7 us -> none  [the longest x1 11.8 us: local(): lax.all_gather(values, 'seq', axis=0, tiled=True)]
    all_to_all x1 -> x0, waiting for transfers between devices: 19.4 us -> none  [local(): lax.all_to_all(replies, 'table', split_axis=0, concat_axis=0, tiled=True)]
    dot_general x10 -> x0, matrix products: 15.6 us -> none  [the longest x2 4.63 us: pair_products(): jnp.einsum('qhe,khe->hqk', split_heads(left_rows), split_heads(right_rows...]
    reshape x11 -> x0, local copies, waits for them, and re-layouts: 8.1 us -> none  [the longest x2 3.86 us: spread_queries(): return summed.reshape(summed.shape[0], -1)]
  transfers between devices with their start and end apart: 3 -> 0, of which waited for: 3 -> 0; matrix products, arithmetic and copies ran while one was open for 2% -> 0% of each run, Pallas kernels for 0% -> 0%
where the time goes in v1:
time: 110 us; the launch traced here: 109 us
  Pallas kernels  100 us (91%)
  local copies, waits for them, and re-layouts  8.16 us (7%)
    pallas_call x1, Pallas kernels, local(): pl.pallas_call(functools.partial(kernel, ring), out_shape=(jax.ShapeDtype...  100 us
    unnamed x16, local copies, waits for them, and re-layouts  8.16 us

profile of v1, /device:TPU:1, one launch (start us, length us, event | category | flops | bytes accessed | tf_op | source)
XLA Modules:
  0.0 109.3 jit_solution(1687964484249509146)
XLA Ops:
  0.6 0.0 copy-start
  0.6 1.6 %copy-done = bf16[512,2048]{1,0:T(8,128)(2,1)S(1)} copy-done((bf16[512,2048]{1,0:T(8,128)(2,1)S(1)}, bf16[512,2048]{1,0:T(8,128)(2,1)}, u32[]{:S(2)}) %copy-start) | copy-done | bytes 2097176
  2.2 0.0 copy-start.1
  2.2 1.0 copy-done.1
  3.3 0.0 copy-start.2
  3.3 1.0 copy-done.2
  4.3 0.0 copy-start.3
  4.3 0.9 copy-done.3
  5.2 0.0 copy-start.4
  5.2 0.7 copy-done.4
  5.9 0.0 copy-start.5
  5.9 0.7 copy-done.5
  6.5 0.0 copy-start.6
  6.5 0.7 copy-done.6
  7.2 100.5 %hstu_step.1 = (bf16[128,512]{1,0:T(8,128)(2,1)S(1)}, f32[512,512]{1,0:T(8,128)S(1)}) custom-call(s32[1,128]{1,0:T(1,128)S(1)} %bitcast.2, s32[1,128]{1,0:T(1,128)S(1)} %bitcast.3, s32[1,3]{1,0:T(1,128)S(1)} %copy-done.6, bf16[512,512]{1,0:T(8,128)(2,1)S(1)} %copy-done.1, bf16[512,2048]{1,0:T(8,128)(2,1)S(1)} %copy-done, bf16[512,512]{1,0:T(8,128)(2,1)S(1)} %copy-done.2, ...), custom_call_target="tpu_custom_call" | custom-call | tf_op jit(solution)/shard_map/hstu_step/pallas_call | solution.py:487
  107.7 0.7 copy.11
  108.3 1.0 copy.12
Async XLA Ops:
  0.6 1.6 %copy-start = (bf16[512,2048]{1,0:T(8,128)(2,1)S(1)}, bf16[512,2048]{1,0:T(8,128)(2,1)}, u32[]{:S(2)}) copy-start(bf16[512,2048]{1,0:T(8,128)(2,1)} %w_in_hbm.1) | copy-start | bytes 6291460
  2.2 1.0 copy-start.1
  3.3 1.0 copy-start.2
  4.3 0.9 copy-start.3
  5.2 0.7 copy-start.4
  5.9 0.7 copy-start.5
  6.5 0.7 copy-start.6

commit v2 on v1

--- a/solution.py
+++ b/solution.py
@@ -29,15 +29,18 @@
 
 def kernel(
     ring,
-    owner_ref,
-    offset_ref,
-    lengths_ref,
+    owner_hbm,
+    offset_hbm,
+    lengths_hbm,
     table_hbm,
     w_in_hbm,
     w_out_hbm,
     up_hbm,
-    layer_hbm,
-    grad_hbm,
+    layer_ref,
+    grad_ref,
+    owner_v,
+    offset_v,
+    lengths,
     id_near,
     id_all,
     slot_rows,
@@ -70,8 +73,6 @@
     g_z,
     g_x,
     g_in,
-    layer_v,
-    grad_v,
     local_sem,
     send_sem,
     recv_sem,
@@ -88,14 +89,34 @@
     z = me // PEERS
     p = me % PEERS
 
+    chip = p // 2
+    core = p % 2
+
+    def near_index(step):
+        over, flip = ((1, 0), (3, 0), (1, 1), (3, 1), (2, 0), (2, 1), (0, 1))[step]
+        return ((chip + over) % (PEERS // 2)) * 2 + (core + flip) % 2
+
     def near(step):
-        return (z * PEERS + (p + step) % PEERS, seq)
-
-    def far(step):
-        return (((z + step) % ring) * PEERS + p, seq)
+        return (z * PEERS + near_index(step), seq)
+
+    def turn(i):
+        hops = (ring - i) // 2
+        odd = i % 2
+        return z + odd * hops + (1 - odd) * (ring - hops)
+
+    def far_index(i):
+        return turn(i) % ring
+
+    def far(i):
+        return (far_index(i) * PEERS + p, seq)
+
+    def beside_index(step):
+        return (seq + (1, 3, 2)[step]) % HEADS
 
     def beside(step):
-        return (me, (seq + step) % HEADS)
+        return (me, beside_index(step))
+
+    leaving = []
 
     def send(src, dst, group, device):
         pltpu.make_async_remote_copy(
@@ -113,15 +134,40 @@
     def rows(start, size):
         return pl.ds(pl.multiple_of(start, size), size)
 
-    ID_NEAR, ID_FAR, UP, SLOTS, SUMS, GATED = range(6)
-    GP = 6
-    Z0 = 10
+    ID_NEAR, ID_FAR, SLOTS, SUMS, GATED = range(5)
+    GP = 5
+    UP = 9
+    Z0 = 12
     X0 = Z0 + PARTS
-    Y0 = X0 + PARTS
-    GZ0 = Y0 + PARTS
+    GZ0 = X0 + PARTS
     GX0 = GZ0 + PARTS
-    GY0 = GX0 + PARTS
-
+    Y0 = GX0 + PARTS
+    GY0 = Y0 + 3 * PARTS
+
+    def spread(buf, start, size, group):
+        mine = rows(start + seq * size, size)
+        for way in (0, 1):
+            send(buf.at[mine, :], buf.at[mine, :], group + way, beside(way))
+            leaving.append((group + way, buf.at[pl.ds(start, size), :]))
+
+    def relay(buf, start, size, group):
+        half = size // 2
+        for way in (0, 1):
+            await_bytes(buf.at[pl.ds(start, size), :], recv_sem.at[group + way])
+            block_of = beside_index(1 - way)
+            here = rows(start + block_of * size + way * half, half)
+            send(buf.at[here, :], buf.at[here, :], group + 2, beside(way))
+        leaving.append((group + 2, buf.at[pl.ds(start, size), :]))
+
+    def settle(buf, start, size, group):
+        await_bytes(buf.at[pl.ds(start, size), :], recv_sem.at[group + 2])
+
+    owner_copy = pltpu.make_async_copy(owner_hbm, owner_v, local_sem.at[4])
+    owner_copy.start()
+    offset_copy = pltpu.make_async_copy(offset_hbm, offset_v, local_sem.at[5])
+    offset_copy.start()
+    lengths_copy = pltpu.make_async_copy(lengths_hbm, lengths, local_sem.at[6])
+    lengths_copy.start()
     up_copy = pltpu.make_async_copy(up_hbm, up_all.at[rows(seq * tokens, tokens), :], local_sem.at[0])
     up_copy.start()
     table_copy = pltpu.make_async_copy(table_hbm, table, local_sem.at[1])
@@ -131,28 +177,28 @@
     out_copy = pltpu.make_async_copy(w_out_hbm, w_out, local_sem.at[3])
     out_copy.start()
 
-    owner = owner_ref[...]
-    code = owner * table.shape[0] + offset_ref[...]
-    id_near[p] = jnp.broadcast_to(code, (8, tokens))
-
     barrier = pltpu.get_barrier_semaphore()
-    for step in range(1, PEERS):
+    for step in range(PEERS - 1):
         pl.semaphore_signal(barrier, inc=1, device_id=near(step), device_id_type=pl.DeviceIdType.MESH)
-    for step in range(1, HEADS):
+    for step in range(HEADS - 1):
         pl.semaphore_signal(barrier, inc=1, device_id=beside(step), device_id_type=pl.DeviceIdType.MESH)
 
-    @pl.loop(1, ring)
+    @pl.loop(0, ring - 1)
     def _(step):
         pl.semaphore_signal(barrier, inc=1, device_id=far(step), device_id_type=pl.DeviceIdType.MESH)
 
+    owner_copy.wait()
+    offset_copy.wait()
+    owner = owner_v[...]
+    code = owner * table.shape[0] + offset_v[...]
+    id_near[p] = jnp.broadcast_to(code, (8, tokens))
     pl.semaphore_wait(barrier, PEERS + ring + HEADS - 3)
 
-    for step in range(1, PEERS):
+    for step in range(PEERS - 1):
         send(id_near.at[p], id_near.at[p], ID_NEAR, near(step))
+    leaving.append((ID_NEAR, id_near.at[pl.ds(0, PEERS - 1)]))
     up_copy.wait()
-    for step in range(1, HEADS):
-        mine = up_all.at[rows(seq * tokens, tokens), :]
-        send(mine, mine, UP, beside(step))
+    spread(up_all, 0, tokens, UP)
 
     owner_lane = jnp.broadcast_to(owner.astype(F32), (tokens, tokens))
     owner_sub = owner_lane.T
@@ -176,9 +222,11 @@
     await_bytes(id_near.at[pl.ds(0, PEERS - 1)], recv_sem.at[ID_NEAR])
     id_all[z] = jnp.concatenate([id_near[i, 0:1, :] for i in range(PEERS)], axis=0)
 
-    @pl.loop(1, ring)
+    @pl.loop(0, ring - 1)
     def _(step):
         send(id_all.at[z], id_all.at[z], ID_FAR, far(step))
+
+    leaving.append((ID_FAR, id_all.at[pl.ds(0, ring - 1)]))
 
     in_copy.wait()
     for i in range(4):
@@ -212,10 +260,12 @@
         rows_out[c] = mul_nn(chosen, table[:, c * part : (c + 1) * part]).astype(BF16)
         mine = rows(z * block, block)
 
-        @pl.loop(1, ring)
+        @pl.loop(0, ring - 1)
         def _(step, c=c, mine=mine):
-            there = rows(((z + step) % ring) * block, block)
+            there = rows(far_index(step) * block, block)
             send(rows_out.at[c, there, :], rows_z.at[c, mine, :], Z0 + c, far(step))
+
+        leaving.append((Z0 + c, rows_z.at[c, pl.ds(0, slots - block), :]))
 
         rows_z[c, mine, :] = rows_out[c, mine, :]
 
@@ -227,10 +277,12 @@
     digits = jnp.concatenate([high, slot_off - 16.0 * high], axis=0).astype(BF16)
     moved = mul_nt(digits, regroup)
     slot_rows[seq] = moved[:8] * 16.0 + moved[8:]
-    for step in range(1, HEADS):
+    for step in range(HEADS - 1):
         send(slot_rows.at[seq], slot_rows.at[seq], SLOTS, beside(step))
-
-    await_bytes(up_all.at[pl.ds(0, 3 * tokens), :], recv_sem.at[UP])
+    leaving.append((SLOTS, slot_rows.at[pl.ds(0, HEADS - 1)]))
+
+    relay(up_all, 0, tokens, UP)
+    settle(up_all, 0, tokens, UP)
     grad_gated[...] = mul_nt(w_out[rows(seq * head, head), :], up_all[...])
     up_t[...] = up_all[rows(seq * tokens, tokens), :].astype(F32).T
 
@@ -238,23 +290,27 @@
         await_bytes(src.at[c, pl.ds(0, slots - block), :], recv_sem.at[src_sem + c])
         mid[c] = mul_nn(regroup, src[c]).astype(BF16)
         mine = rows(base + p * chunk_rows, chunk_rows)
-        for step in range(1, PEERS):
-            there = rows(((p + step) % PEERS) * chunk_rows, chunk_rows)
+        for step in range(PEERS - 1):
+            there = rows(near_index(step) * chunk_rows, chunk_rows)
             send(mid.at[c, there, :], dst.at[c, mine, :], sem + c, near(step))
+        leaving.append((sem + c, dst.at[c, pl.ds(0, slots - chunk_rows), :]))
         dst[c, mine, :] = mid[c, rows(p * chunk_rows, chunk_rows), :]
 
     def gather_rows(c):
         await_bytes(rows_in.at[c, pl.ds(0, slots - chunk_rows), :], recv_sem.at[X0 + c])
         mine = rows(seq * tokens, tokens)
         emb_all[c, mine, :] = mul_nn(pick_in, rows_in[c]).astype(BF16)
-        for step in range(1, HEADS):
-            send(emb_all.at[c, mine, :], emb_all.at[c, mine, :], Y0 + c, beside(step))
+        spread(emb_all.at[c], 0, tokens, Y0 + 3 * c)
 
     for c in range(PARTS):
         pass_near(c, rows_z, Z0, rows_x, rows_in, 0, X0)
         if c > 0:
             gather_rows(c - 1)
+        if c > 1:
+            relay(emb_all.at[c - 2], 0, tokens, Y0 + 3 * (c - 2))
     gather_rows(PARTS - 1)
+    for c in range(max(0, PARTS - 2), PARTS):
+        relay(emb_all.at[c], 0, tokens, Y0 + 3 * c)
 
     own = rows(seq * tokens, tokens)
     emb_own = jnp.concatenate([emb_all[c, own, :] for c in range(PARTS)], axis=1).astype(F32)
@@ -264,7 +320,7 @@
     normed_t[...] = centered_t * inv_own
 
     for c in range(PARTS):
-        await_bytes(emb_all.at[c, pl.ds(0, 3 * tokens), :], recv_sem.at[Y0 + c])
+        settle(emb_all.at[c], 0, tokens, Y0 + 3 * c)
     for i in range(HEADS):
         here = slice(i * tokens, (i + 1) * tokens)
         wide = jnp.concatenate([emb_all[c, here, :] for c in range(PARTS)], axis=1).astype(F32)
@@ -284,8 +340,9 @@
     kv_rows[0] = act[value, :].T
     kv_rows[1] = act[key, :].T
 
-    start_two = lengths_ref[0, 0]
-    start_three = start_two + lengths_ref[0, 1]
+    lengths_copy.wait()
+    start_two = lengths[0, 0]
+    start_three = start_two + lengths[0, 1]
 
     def user_of(position):
         return (position >= start_two).astype(jnp.int32) + (position >= start_three).astype(jnp.int32)
@@ -323,8 +380,9 @@
         sums[seq, :, here] = jnp.concatenate(
             [out_mean, out_sq, g_mean, cross, jnp.zeros((4, tokens), F32)], axis=0
         )
-    for step in range(1, HEADS):
+    for step in range(HEADS - 1):
         send(sums.at[seq], sums.at[seq], SUMS, beside(step))
+    leaving.append((SUMS, sums.at[pl.ds(0, HEADS - 1)]))
 
     await_bytes(sums.at[pl.ds(0, HEADS - 1)], recv_sem.at[SUMS])
     parts = [sums[i] for i in range(HEADS)]
@@ -347,9 +405,10 @@
     def exchange(i):
         here = pl.ds(i * head, head)
         mine = pl.ds(pl.multiple_of(i * width + seq * head, head), head)
-        for step in range(1, HEADS):
-            there = (seq + step) % HEADS
+        for step in range(HEADS - 1):
+            there = beside_index(step)
             send(gp_out.at[there, here, :], gp_in.at[mine, :], GP + i, beside(step))
+        leaving.append((GP + i, gp_in.at[pl.ds(i * width, 3 * head), :]))
         gp_in[mine, :] = gp_out[seq, here, :]
 
     grad_out = []
@@ -368,8 +427,9 @@
         )
     exchange(0)
     mine = rows(seq * head, head)
-    for step in range(1, HEADS):
-        send(gated_out.at[(seq + step) % HEADS], gated_in.at[mine, :], GATED, beside(step))
+    for step in range(HEADS - 1):
+        send(gated_out.at[beside_index(step)], gated_in.at[mine, :], GATED, beside(step))
+    leaving.append((GATED, gated_in.at[pl.ds(0, 3 * head), :]))
     gated_in[mine, :] = gated_out[seq]
     grad_out = jnp.concatenate(grad_out, axis=1)
     for i in range(HEADS):
@@ -409,21 +469,21 @@
         g_out[c] = mul_nt(place_out, grad_rows[c * part : (c + 1) * part]).astype(BF16)
         mine = rows(z * block, block)
 
-        @pl.loop(1, ring)
+        @pl.loop(0, ring - 1)
         def _(step, c=c, mine=mine):
-            there = rows(((z + step) % ring) * block, block)
+            there = rows(far_index(step) * block, block)
             send(g_out.at[c, there, :], g_z.at[c, mine, :], GZ0 + c, far(step))
 
+        leaving.append((GZ0 + c, g_z.at[c, pl.ds(0, slots - block), :]))
+
         g_z[c, mine, :] = g_out[c, mine, :]
 
     await_bytes(gated_in.at[pl.ds(0, 3 * head), :], recv_sem.at[GATED])
-    layer_v[...] = (emb_own + mul_nn(gated_in[...].T, w_out[...])).astype(BF16)
-    layer_copy = pltpu.make_async_copy(layer_v, layer_hbm, local_sem.at[4])
-    layer_copy.start()
+    layer_ref[...] = (emb_own + mul_nn(gated_in[...].T, w_out[...])).astype(BF16)
 
     await_bytes(slot_rows.at[pl.ds(0, HEADS - 1)], recv_sem.at[SLOTS])
     table_row = iota((table.shape[0], slots), 0).astype(F32)
-    spread = jnp.concatenate(
+    placed = jnp.concatenate(
         [
             jnp.where(table_row == slot_rows[i, 0:1, :], 1.0, 0.0).astype(BF16)
             for i in range(HEADS)
@@ -432,44 +492,24 @@
     )
 
     def pass_beside(c):
-        mine = rows(seq * slots, slots)
         await_bytes(g_in.at[c, pl.ds(0, slots - chunk_rows), :], recv_sem.at[GX0 + c])
-        for step in range(1, HEADS):
-            send(g_in.at[c, mine, :], g_in.at[c, mine, :], GY0 + c, beside(step))
+        spread(g_in.at[c], 0, slots, GY0 + 3 * c)
 
     for c in range(PARTS):
         pass_near(c, g_z, GZ0, g_x, g_in, seq * slots, GX0)
         if c > 0:
             pass_beside(c - 1)
+        if c > 1:
+            relay(g_in.at[c - 2], 0, slots, GY0 + 3 * (c - 2))
     pass_beside(PARTS - 1)
-    grad_copies = []
+    for c in range(max(0, PARTS - 2), PARTS):
+        relay(g_in.at[c], 0, slots, GY0 + 3 * c)
     for c in range(PARTS):
-        await_bytes(g_in.at[c, pl.ds(0, 3 * slots), :], recv_sem.at[GY0 + c])
-        grad_v[c] = mul_nn(spread, g_in[c])
-        copy = pltpu.make_async_copy(
-            grad_v.at[c], grad_hbm.at[:, pl.ds(c * part, part)], local_sem.at[5 + c]
-        )
-        copy.start()
-        grad_copies.append(copy)
-
-    await_bytes(id_near.at[pl.ds(0, PEERS - 1)], send_sem.at[ID_NEAR])
-    await_bytes(id_all.at[pl.ds(0, ring - 1)], send_sem.at[ID_FAR])
-    await_bytes(up_all.at[pl.ds(0, 3 * tokens), :], send_sem.at[UP])
-    await_bytes(slot_rows.at[pl.ds(0, HEADS - 1)], send_sem.at[SLOTS])
-    await_bytes(sums.at[pl.ds(0, HEADS - 1)], send_sem.at[SUMS])
-    await_bytes(gated_in.at[pl.ds(0, 3 * head), :], send_sem.at[GATED])
-    for i in range(4):
-        await_bytes(gp_in.at[pl.ds(i * width, 3 * head), :], send_sem.at[GP + i])
-    for c in range(PARTS):
-        await_bytes(rows_z.at[c, pl.ds(0, slots - block), :], send_sem.at[Z0 + c])
-        await_bytes(rows_in.at[c, pl.ds(0, slots - chunk_rows), :], send_sem.at[X0 + c])
-        await_bytes(emb_all.at[c, pl.ds(0, 3 * tokens), :], send_sem.at[Y0 + c])
-        await_bytes(g_z.at[c, pl.ds(0, slots - block), :], send_sem.at[GZ0 + c])
-        await_bytes(g_in.at[c, pl.ds(0, slots - chunk_rows), :], send_sem.at[GX0 + c])
-        await_bytes(g_in.at[c, pl.ds(0, 3 * slots), :], send_sem.at[GY0 + c])
-    layer_copy.wait()
-    for copy in grad_copies:
-        copy.wait()
+        settle(g_in.at[c], 0, slots, GY0 + 3 * c)
+        grad_ref[:, c * part : (c + 1) * part] = mul_nn(placed, g_in[c])
+
+    for group, view in leaving:
+        await_bytes(view, send_sem.at[group])
 
 
 def local(embedding_table, project_in, project_out, row_owner, row_offset, user_lengths, upstream):
@@ -480,19 +520,21 @@
     slots = 2 * PEERS * ring
     part = width // PARTS
     head = width // HEADS
-    any_spec = pl.BlockSpec(memory_space=pl.ANY)
     vmem_spec = pl.BlockSpec(memory_space=pltpu.VMEM)
-    smem_spec = pl.BlockSpec(memory_space=pltpu.SMEM)
+    hbm_spec = pl.BlockSpec(memory_space=pltpu.HBM)
     vmem = pltpu.VMEM
     return pl.pallas_call(
         functools.partial(kernel, ring),
         out_shape=(
-            jax.ShapeDtypeStruct((tokens, width), BF16),
-            jax.ShapeDtypeStruct((table_rows, width), F32),
+            vmem((tokens, width), BF16),
+            vmem((table_rows, width), F32),
         ),
-        in_specs=[vmem_spec, vmem_spec, smem_spec] + [any_spec] * 4,
-        out_specs=(any_spec, any_spec),
+        in_specs=[hbm_spec] * 7,
+        out_specs=(vmem_spec, vmem_spec),
         scratch_shapes=[
+            vmem((1, tokens), jnp.int32),
+            vmem((1, tokens), jnp.int32),
+            pltpu.SMEM((1, 3), jnp.int32),
             vmem((PEERS, 8, tokens), jnp.int32),
             vmem((ring, PEERS, tokens), jnp.int32),
             vmem((HEADS, 8, slots), F32),
@@ -525,14 +567,12 @@
             vmem((PARTS, slots, part), BF16),
             vmem((PARTS, slots, part), BF16),
             vmem((PARTS, HEADS * slots, part), BF16),
-            vmem((tokens, width), BF16),
-            vmem((PARTS, table_rows, part), F32),
-            pltpu.SemaphoreType.DMA((5 + PARTS,)),
-            pltpu.SemaphoreType.DMA((10 + 6 * PARTS,)),
-            pltpu.SemaphoreType.DMA((10 + 6 * PARTS,)),
+            pltpu.SemaphoreType.DMA((7,)),
+            pltpu.SemaphoreType.DMA((12 + 10 * PARTS,)),
+            pltpu.SemaphoreType.DMA((12 + 10 * PARTS,)),
         ],
         compiler_params=pltpu.CompilerParams(
-            collective_id=0, has_side_effects=True, vmem_limit_bytes=48 * 2**20
+            collective_id=0, has_side_effects=True, vmem_limit_bytes=58 * 2**20
         ),
         name="hstu_step",
     )(

time: 110 us -> 95.3 us (0.87)
  Pallas kernels: 100 us -> 92.7 us
  local copies, waits for them, and re-layouts: 8.16 us -> 1.63 us
    pallas_call x1, Pallas kernels: 100 us -> 92.7 us  [local(): pl.pallas_call(functools.partial(kernel, ring), out_shape=(vmem((tokens,...]
    unnamed x16 -> x2, local copies, waits for them, and re-layouts: 8.16 us -> 1.63 us
where the time goes in v2:
time: 95.3 us; the launch traced here: 95 us
  Pallas kernels  92.7 us (97%)
  local copies, waits for them, and re-layouts  1.63 us (2%)
    pallas_call x1, Pallas kernels, local(): pl.pallas_call(functools.partial(kernel, ring), out_shape=(vmem((tokens,...  92.7 us

profile of v2, /device:TPU:1, one launch (start us, length us, event | category | flops | bytes accessed | tf_op | source)
XLA Modules:
  0.0 95.0 jit_solution(5264842177348038925)
XLA Ops:
  0.6 92.7 %hstu_step.1 = (bf16[128,512]{1,0:T(8,128)(2,1)S(1)}, f32[512,512]{1,0:T(8,128)S(1)}) custom-call(s32[1,128]{1,0:T(1,128)} %bitcast.2, s32[1,128]{1,0:T(1,128)} %bitcast.3, s32[1,3]{1,0:T(1,128)} %lengths_hbm.1, bf16[512,512]{1,0:T(8,128)(2,1)} %table_hbm.1, bf16[512,2048]{1,0:T(8,128)(2,1)} %w_in_hbm.1, bf16[512,512]{1,0:T(8,128)(2,1)} %w_out_hbm.1, ...), custom_call_target="tpu_custom_call" | custom-call | tf_op jit(solution)/shard_map/hstu_step/pallas_call | solution.py:526
  93.4 0.7 copy.11
  94.0 1.0 %copy.12 = f32[512,512]{1,0:T(8,128)} copy(f32[512,512]{1,0:T(8,128)S(1)} %get-tuple-element.3) | data formatting | bytes 2097152

commit v3 on v2

--- a/solution.py
+++ b/solution.py
@@ -10,7 +10,8 @@
 HEADS = 4
 EPS = 1e-05
 PEERS = 8
-PARTS = 2
+ROW_PARTS = 4
+GRAD_PARTS = 4
 F32 = jnp.float32
 BF16 = jnp.bfloat16
 
@@ -80,7 +81,8 @@
     tokens = 128
     width = table.shape[1]
     head = width // HEADS
-    part = width // PARTS
+    row_part = width // ROW_PARTS
+    grad_part = width // GRAD_PARTS
     slots = 2 * PEERS * ring
     block = 2 * PEERS
     chunk_rows = 2 * ring
@@ -93,11 +95,16 @@
     core = p % 2
 
     def near_index(step):
-        over, flip = ((1, 0), (3, 0), (1, 1), (3, 1), (2, 0), (2, 1), (0, 1))[step]
+        over, flip = ((1, 0), (3, 0), (1, 1), (3, 1), (2, 0), (2, 1), (0, 1), (0, 0))[step]
         return ((chip + over) % (PEERS // 2)) * 2 + (core + flip) % 2
 
     def near(step):
         return (z * PEERS + near_index(step), seq)
+
+    around = [(near, beside) for beside in (2, 0, 1) for near in (4, 5, 0, 1, 2, 3, 6)]
+    around = around[:2] + around[7:9] + around[14:16] + around[2:7] + around[9:14] + around[16:]
+    around += [(near, 3) for near in range(PEERS - 1)]
+    around += [(PEERS - 1, beside) for beside in (2, 0, 1)]
 
     def turn(i):
         hops = (ring - i) // 2
@@ -111,7 +118,7 @@
         return (far_index(i) * PEERS + p, seq)
 
     def beside_index(step):
-        return (seq + (1, 3, 2)[step]) % HEADS
+        return (seq + (1, 3, 2, 0)[step]) % HEADS
 
     def beside(step):
         return (me, beside_index(step))
@@ -137,30 +144,20 @@
     ID_NEAR, ID_FAR, SLOTS, SUMS, GATED = range(5)
     GP = 5
     UP = 9
-    Z0 = 12
-    X0 = Z0 + PARTS
-    GZ0 = X0 + PARTS
-    GX0 = GZ0 + PARTS
-    Y0 = GX0 + PARTS
-    GY0 = Y0 + 3 * PARTS
-
-    def spread(buf, start, size, group):
+    Z0 = 10
+    X0 = Z0 + ROW_PARTS
+    Y0 = X0 + ROW_PARTS
+    GZ0 = Y0 + ROW_PARTS
+    GX0 = GZ0 + GRAD_PARTS
+
+    def spread_all(buf, start, size, group):
         mine = rows(start + seq * size, size)
-        for way in (0, 1):
-            send(buf.at[mine, :], buf.at[mine, :], group + way, beside(way))
-            leaving.append((group + way, buf.at[pl.ds(start, size), :]))
-
-    def relay(buf, start, size, group):
-        half = size // 2
-        for way in (0, 1):
-            await_bytes(buf.at[pl.ds(start, size), :], recv_sem.at[group + way])
-            block_of = beside_index(1 - way)
-            here = rows(start + block_of * size + way * half, half)
-            send(buf.at[here, :], buf.at[here, :], group + 2, beside(way))
-        leaving.append((group + 2, buf.at[pl.ds(start, size), :]))
-
-    def settle(buf, start, size, group):
-        await_bytes(buf.at[pl.ds(start, size), :], recv_sem.at[group + 2])
+        for step in range(HEADS - 1):
+            send(buf.at[mine, :], buf.at[mine, :], group, beside(step))
+        leaving.append((group, buf.at[pl.ds(start, 3 * size), :]))
+
+    def settle_all(buf, start, size, group):
+        await_bytes(buf.at[pl.ds(start, 3 * size), :], recv_sem.at[group])
 
     owner_copy = pltpu.make_async_copy(owner_hbm, owner_v, local_sem.at[4])
     owner_copy.start()
@@ -178,10 +175,9 @@
     out_copy.start()
 
     barrier = pltpu.get_barrier_semaphore()
-    for step in range(PEERS - 1):
-        pl.semaphore_signal(barrier, inc=1, device_id=near(step), device_id_type=pl.DeviceIdType.MESH)
-    for step in range(HEADS - 1):
-        pl.semaphore_signal(barrier, inc=1, device_id=beside(step), device_id_type=pl.DeviceIdType.MESH)
+    for one, two in around:
+        there = (z * PEERS + near_index(one), beside_index(two))
+        pl.semaphore_signal(barrier, inc=1, device_id=there, device_id_type=pl.DeviceIdType.MESH)
 
     @pl.loop(0, ring - 1)
     def _(step):
@@ -192,13 +188,11 @@
     owner = owner_v[...]
     code = owner * table.shape[0] + offset_v[...]
     id_near[p] = jnp.broadcast_to(code, (8, tokens))
-    pl.semaphore_wait(barrier, PEERS + ring + HEADS - 3)
+    pl.semaphore_wait(barrier, len(around) + ring - 1)
 
     for step in range(PEERS - 1):
         send(id_near.at[p], id_near.at[p], ID_NEAR, near(step))
     leaving.append((ID_NEAR, id_near.at[pl.ds(0, PEERS - 1)]))
-    up_copy.wait()
-    spread(up_all, 0, tokens, UP)
 
     owner_lane = jnp.broadcast_to(owner.astype(F32), (tokens, tokens))
     owner_sub = owner_lane.T
@@ -227,6 +221,8 @@
         send(id_all.at[z], id_all.at[z], ID_FAR, far(step))
 
     leaving.append((ID_FAR, id_all.at[pl.ds(0, ring - 1)]))
+    up_copy.wait()
+    spread_all(up_all, 0, tokens, UP)
 
     in_copy.wait()
     for i in range(4):
@@ -256,8 +252,8 @@
     chosen = interleave(
         jnp.where(row_id == first_off, 1.0, 0.0), jnp.where(row_id == last_off, 1.0, 0.0)
     ).astype(BF16)
-    for c in range(PARTS):
-        rows_out[c] = mul_nn(chosen, table[:, c * part : (c + 1) * part]).astype(BF16)
+    for c in range(ROW_PARTS):
+        rows_out[c] = mul_nn(chosen, table[:, c * row_part : (c + 1) * row_part]).astype(BF16)
         mine = rows(z * block, block)
 
         @pl.loop(0, ring - 1)
@@ -281,8 +277,7 @@
         send(slot_rows.at[seq], slot_rows.at[seq], SLOTS, beside(step))
     leaving.append((SLOTS, slot_rows.at[pl.ds(0, HEADS - 1)]))
 
-    relay(up_all, 0, tokens, UP)
-    settle(up_all, 0, tokens, UP)
+    settle_all(up_all, 0, tokens, UP)
     grad_gated[...] = mul_nt(w_out[rows(seq * head, head), :], up_all[...])
     up_t[...] = up_all[rows(seq * tokens, tokens), :].astype(F32).T
 
@@ -300,30 +295,26 @@
         await_bytes(rows_in.at[c, pl.ds(0, slots - chunk_rows), :], recv_sem.at[X0 + c])
         mine = rows(seq * tokens, tokens)
         emb_all[c, mine, :] = mul_nn(pick_in, rows_in[c]).astype(BF16)
-        spread(emb_all.at[c], 0, tokens, Y0 + 3 * c)
-
-    for c in range(PARTS):
+        spread_all(emb_all.at[c], 0, tokens, Y0 + c)
+
+    for c in range(ROW_PARTS):
         pass_near(c, rows_z, Z0, rows_x, rows_in, 0, X0)
         if c > 0:
             gather_rows(c - 1)
-        if c > 1:
-            relay(emb_all.at[c - 2], 0, tokens, Y0 + 3 * (c - 2))
-    gather_rows(PARTS - 1)
-    for c in range(max(0, PARTS - 2), PARTS):
-        relay(emb_all.at[c], 0, tokens, Y0 + 3 * c)
+    gather_rows(ROW_PARTS - 1)
 
     own = rows(seq * tokens, tokens)
-    emb_own = jnp.concatenate([emb_all[c, own, :] for c in range(PARTS)], axis=1).astype(F32)
+    emb_own = jnp.concatenate([emb_all[c, own, :] for c in range(ROW_PARTS)], axis=1).astype(F32)
     emb_t = emb_own.T
     centered_t = emb_t - jnp.mean(emb_t, axis=0, keepdims=True)
     inv_own = lax.rsqrt(jnp.mean(centered_t * centered_t, axis=0, keepdims=True) + EPS)
     normed_t[...] = centered_t * inv_own
 
-    for c in range(PARTS):
-        settle(emb_all.at[c], 0, tokens, Y0 + 3 * c)
+    for c in range(ROW_PARTS):
+        settle_all(emb_all.at[c], 0, tokens, Y0 + c)
     for i in range(HEADS):
         here = slice(i * tokens, (i + 1) * tokens)
-        wide = jnp.concatenate([emb_all[c, here, :] for c in range(PARTS)], axis=1).astype(F32)
+        wide = jnp.concatenate([emb_all[c, here, :] for c in range(ROW_PARTS)], axis=1).astype(F32)
         centered = wide - jnp.mean(wide, axis=1, keepdims=True)
         inv = lax.rsqrt(jnp.mean(centered * centered, axis=1, keepdims=True) + EPS)
         normed_bf[here, :] = (centered * inv).astype(BF16)
@@ -383,6 +374,11 @@
     for step in range(HEADS - 1):
         send(sums.at[seq], sums.at[seq], SUMS, beside(step))
     leaving.append((SUMS, sums.at[pl.ds(0, HEADS - 1)]))
+    for i in range(4):
+        here = slice(i * head, (i + 1) * head)
+        x = pre[here, :]
+        logistic = jax.nn.sigmoid(x)
+        pre[here, :] = logistic * (1.0 + x * (1.0 - logistic))
 
     await_bytes(sums.at[pl.ds(0, HEADS - 1)], recv_sem.at[SUMS])
     parts = [sums[i] for i in range(HEADS)]
@@ -398,9 +394,7 @@
     slant = inv_out * cross * (1.0 / width)
 
     def pre_slope(part_of, here):
-        x = pre[part_of, here]
-        logistic = jax.nn.sigmoid(x)
-        return logistic * (1.0 + x * (1.0 - logistic))
+        return pre[part_of, here]
 
     def exchange(i):
         here = pl.ds(i * head, head)
@@ -426,11 +420,6 @@
             ).astype(BF16)
         )
     exchange(0)
-    mine = rows(seq * head, head)
-    for step in range(HEADS - 1):
-        send(gated_out.at[beside_index(step)], gated_in.at[mine, :], GATED, beside(step))
-    leaving.append((GATED, gated_in.at[pl.ds(0, 3 * head), :]))
-    gated_in[mine, :] = gated_out[seq]
     grad_out = jnp.concatenate(grad_out, axis=1)
     for i in range(HEADS):
         ns = queries_of(i)
@@ -452,6 +441,11 @@
         found = mul_nt(act[query, ns], weights[blocks[i], ns])
         gp_out[i, key, :] = (found * pre_slope(key, blocks[i])).astype(BF16)
     exchange(3)
+    mine = rows(seq * head, head)
+    for step in range(HEADS - 1):
+        send(gated_out.at[beside_index(step)], gated_in.at[mine, :], GATED, beside(step))
+    leaving.append((GATED, gated_in.at[pl.ds(0, 3 * head), :]))
+    gated_in[mine, :] = gated_out[seq]
 
     grad_normed = jnp.zeros((width, tokens), F32)
     for i in range(4):
@@ -465,8 +459,8 @@
         - normed * jnp.mean(grad_normed * normed, axis=0, keepdims=True)
     )
     grad_rows = grad_rows.astype(BF16)
-    for c in range(PARTS):
-        g_out[c] = mul_nt(place_out, grad_rows[c * part : (c + 1) * part]).astype(BF16)
+    for c in range(GRAD_PARTS):
+        g_out[c] = mul_nt(place_out, grad_rows[c * grad_part : (c + 1) * grad_part]).astype(BF16)
         mine = rows(z * block, block)
 
         @pl.loop(0, ring - 1)
@@ -491,22 +485,20 @@
         axis=1,
     )
 
-    def pass_beside(c):
-        await_bytes(g_in.at[c, pl.ds(0, slots - chunk_rows), :], recv_sem.at[GX0 + c])
-        spread(g_in.at[c], 0, slots, GY0 + 3 * c)
-
-    for c in range(PARTS):
-        pass_near(c, g_z, GZ0, g_x, g_in, seq * slots, GX0)
-        if c > 0:
-            pass_beside(c - 1)
-        if c > 1:
-            relay(g_in.at[c - 2], 0, slots, GY0 + 3 * (c - 2))
-    pass_beside(PARTS - 1)
-    for c in range(max(0, PARTS - 2), PARTS):
-        relay(g_in.at[c], 0, slots, GY0 + 3 * c)
-    for c in range(PARTS):
-        settle(g_in.at[c], 0, slots, GY0 + 3 * c)
-        grad_ref[:, c * part : (c + 1) * part] = mul_nn(placed, g_in[c])
+    mine = rows(seq * slots + p * chunk_rows, chunk_rows)
+    for c in range(GRAD_PARTS):
+        await_bytes(g_z.at[c, pl.ds(0, slots - block), :], recv_sem.at[GZ0 + c])
+        g_x[c] = mul_nn(regroup, g_z[c]).astype(BF16)
+        for one, two in around:
+            to = near_index(one)
+            there = rows(to * chunk_rows, chunk_rows)
+            device = (z * PEERS + to, beside_index(two))
+            send(g_x.at[c, there, :], g_in.at[c, mine, :], GX0 + c, device)
+        leaving.append((GX0 + c, g_in.at[c, pl.ds(0, HEADS * slots - chunk_rows), :]))
+        g_in[c, mine, :] = g_x[c, rows(p * chunk_rows, chunk_rows), :]
+    for c in range(GRAD_PARTS):
+        await_bytes(g_in.at[c, pl.ds(0, HEADS * slots - chunk_rows), :], recv_sem.at[GX0 + c])
+        grad_ref[:, c * grad_part : (c + 1) * grad_part] = mul_nn(placed, g_in[c])
 
     for group, view in leaving:
         await_bytes(view, send_sem.at[group])
@@ -518,7 +510,6 @@
     ring = lax.axis_size("table") // PEERS
     group = tokens * HEADS
     slots = 2 * PEERS * ring
-    part = width // PARTS
     head = width // HEADS
     vmem_spec = pl.BlockSpec(memory_space=pltpu.VMEM)
     hbm_spec = pl.BlockSpec(memory_space=pltpu.HBM)
@@ -543,11 +534,11 @@
             vmem((width, width), BF16),
             vmem((group, width), BF16),
             vmem((4 * head, width), BF16),
-            vmem((PARTS, slots, part), BF16),
-            vmem((PARTS, slots, part), BF16),
-            vmem((PARTS, slots, part), BF16),
-            vmem((PARTS, slots, part), BF16),
-            vmem((PARTS, group, part), BF16),
+            vmem((ROW_PARTS, slots, width // ROW_PARTS), BF16),
+            vmem((ROW_PARTS, slots, width // ROW_PARTS), BF16),
+            vmem((ROW_PARTS, slots, width // ROW_PARTS), BF16),
+            vmem((ROW_PARTS, slots, width // ROW_PARTS), BF16),
+            vmem((ROW_PARTS, group, width // ROW_PARTS), BF16),
             vmem((group, width), BF16),
             vmem((4 * head, group), F32),
             vmem((4 * head, group), BF16),
@@ -563,13 +554,13 @@
             vmem((4 * width, tokens), BF16),
             vmem((width, tokens), F32),
             vmem((width, tokens), F32),
-            vmem((PARTS, slots, part), BF16),
-            vmem((PARTS, slots, part), BF16),
-            vmem((PARTS, slots, part), BF16),
-            vmem((PARTS, HEADS * slots, part), BF16),
+            vmem((GRAD_PARTS, slots, width // GRAD_PARTS), BF16),
+            vmem((GRAD_PARTS, slots, width // GRAD_PARTS), BF16),
+            vmem((GRAD_PARTS, slots, width // GRAD_PARTS), BF16),
+            vmem((GRAD_PARTS, HEADS * slots, width // GRAD_PARTS), BF16),
             pltpu.SemaphoreType.DMA((7,)),
-            pltpu.SemaphoreType.DMA((12 + 10 * PARTS,)),
-            pltpu.SemaphoreType.DMA((12 + 10 * PARTS,)),
+            pltpu.SemaphoreType.DMA((10 + 3 * ROW_PARTS + 2 * GRAD_PARTS,)),
+            pltpu.SemaphoreType.DMA((10 + 3 * ROW_PARTS + 2 * GRAD_PARTS,)),
         ],
         compiler_params=pltpu.CompilerParams(
             collective_id=0, has_side_effects=True, vmem_limit_bytes=58 * 2**20

time: 95.3 us -> 87.4 us (0.917)
  Pallas kernels: 92.7 us -> 85 us
    pallas_call x1, Pallas kernels: 92.7 us -> 85 us  [local(): pl.pallas_call(functools.partial(kernel, ring), out_shape=(vmem((tokens,...]
where the time goes in v3:
time: 87.4 us; the launch traced here: 87.3 us
  Pallas kernels  85 us (97%)
  local copies, waits for them, and re-layouts  1.63 us (2%)
    pallas_call x1, Pallas kernels, local(): pl.pallas_call(functools.partial(kernel, ring), out_shape=(vmem((tokens,...  85 us

profile of v3, /device:TPU:1, one launch (start us, length us, event | category | flops | bytes accessed | tf_op | source)
XLA Modules:
  0.0 87.3 jit_solution(4843968556189181323)
XLA Ops:
  0.6 85.0 %hstu_step.1 = (bf16[128,512]{1,0:T(8,128)(2,1)S(1)}, f32[512,512]{1,0:T(8,128)S(1)}) custom-call(s32[1,128]{1,0:T(1,128)} %bitcast.2, s32[1,128]{1,0:T(1,128)} %bitcast.3, s32[1,3]{1,0:T(1,128)} %lengths_hbm.1, bf16[512,512]{1,0:T(8,128)(2,1)} %table_hbm.1, bf16[512,2048]{1,0:T(8,128)(2,1)} %w_in_hbm.1, bf16[512,512]{1,0:T(8,128)(2,1)} %w_out_hbm.1, ...), custom_call_target="tpu_custom_call" | custom-call | tf_op jit(solution)/shard_map/hstu_step/pallas_call | solution.py:517
  85.6 0.7 copy.11
  86.3 1.0 %copy.12 = f32[512,512]{1,0:T(8,128)} copy(f32[512,512]{1,0:T(8,128)S(1)} %get-tuple-element.3) | data formatting | bytes 2097152

commit v4 on v3

v4 whole, which is shorter than its diff:
```python
import functools

import jax
import jax.numpy as jnp
from jax import lax
from jax.experimental import pallas as pl
from jax.experimental.pallas import tpu as pltpu
from jax.sharding import PartitionSpec as P

HEADS = 4
EPS = 1e-05
PEERS = 8
ROW_PARTS = 4
GRAD_PARTS = 4
F32 = jnp.float32
BF16 = jnp.bfloat16


def mul_nn(left, right):
    return lax.dot_general(left, right, (((1,), (0,)), ((), ())), preferred_element_type=F32)


def mul_nt(left, right):
    return lax.dot_general(left, right, (((1,), (1,)), ((), ())), preferred_element_type=F32)


def iota(shape, axis):
    return lax.broadcasted_iota(jnp.int32, shape, axis)


def kernel(
    ring,
    owner_hbm,
    offset_hbm,
    lengths_hbm,
    table_hbm,
    w_in_hbm,
    w_out_hbm,
    up_hbm,
    layer_ref,
    grad_ref,
    owner_v,
    offset_v,
    lengths,
    id_near,
    id_seq,
    id_all,
    slot_rows,
    table,
    w_in,
    w_out,
    up_all,
    w_head,
    rows_out,
    rows_z,
    rows_x,
    rows_in,
    emb_all,
    normed_bf,
    pre,
    act,
    kv_rows,
    weights,
    slopes,
    grad_gated,
    attended,
    grad_out,
    gated,
    gp_in,
    normed_t,
    up_t,
    g_out,
    g_z,
    g_x,
    g_in,
    local_sem,
    send_sem,
    recv_sem,
):
    tokens = 128
    width = table.shape[1]
    head = width // HEADS
    row_part = width // ROW_PARTS
    grad_part = width // GRAD_PARTS
    slots = 2 * PEERS * ring
    block = 2 * PEERS
    chunk_rows = 2 * ring
    me = lax.axis_index("table")
    seq = lax.axis_index("seq")
    z = me // PEERS
    p = me % PEERS

    chip = p // 2
    core = p % 2

    def near_index(step):
        over, flip = ((1, 0), (3, 0), (1, 1), (3, 1), (2, 0), (2, 1), (0, 1), (0, 0))[step]
        return ((chip + over) % (PEERS // 2)) * 2 + (core + flip) % 2

    def near(step):
        return (z * PEERS + near_index(step), seq)

    around = [(near, beside) for beside in (2, 0, 1) for near in (4, 5, 0, 1, 2, 3, 6)]
    around = around[:2] + around[7:9] + around[14:16] + around[2:7] + around[9:14] + around[16:]
    around += [(near, 3) for near in range(PEERS - 1)]
    around += [(PEERS - 1, beside) for beside in (2, 0, 1)]

    def turn(i):
        hops = (ring - i) // 2
        odd = i % 2
        return z + odd * hops + (1 - odd) * (ring - hops)

    def far_index(i):
        return turn(i) % ring

    def far(i):
        return (far_index(i) * PEERS + p, seq)

    def beside_index(step):
        return (seq + (1, 3, 2, 0)[step]) % HEADS

    def beside(step):
        return (me, beside_index(step))

    leaving = []

    def send(src, dst, group, device):
        pltpu.make_async_remote_copy(
            src_ref=src,
            dst_ref=dst,
            send_sem=send_sem.at[group],
            recv_sem=recv_sem.at[group],
            device_id=device,
            device_id_type=pl.DeviceIdType.MESH,
        ).start()

    def await_bytes(view, sem):
        pltpu.make_async_copy(view, view, sem).wait()

    def rows(start, size):
        return pl.ds(pl.multiple_of(start, size), size)

    ID_NEAR, ID_FAR, ID_SEQ, SLOTS, UP = range(5)
    Z0 = 5
    X0 = Z0 + ROW_PARTS
    GZ0 = X0 + ROW_PARTS
    GX0 = GZ0 + GRAD_PARTS

    def spread_all(buf, start, size, group):
        mine = rows(start + seq * size, size)
        for step in range(HEADS - 1):
            send(buf.at[mine, :], buf.at[mine, :], group, beside(step))
        leaving.append((group, buf.at[pl.ds(start, 3 * size), :]))

    def settle_all(buf, start, size, group):
        await_bytes(buf.at[pl.ds(start, 3 * size), :], recv_sem.at[group])

    owner_copy = pltpu.make_async_copy(owner_hbm, owner_v, local_sem.at[4])
    owner_copy.start()
    offset_copy = pltpu.make_async_copy(offset_hbm, offset_v, local_sem.at[5])
    offset_copy.start()
    lengths_copy = pltpu.make_async_copy(lengths_hbm, lengths, local_sem.at[6])
    lengths_copy.start()
    up_copy = pltpu.make_async_copy(up_hbm, up_all.at[rows(seq * tokens, tokens), :], local_sem.at[0])
    up_copy.start()
    table_copy = pltpu.make_async_copy(table_hbm, table, local_sem.at[1])
    table_copy.start()
    in_copy = pltpu.make_async_copy(w_in_hbm, w_in, local_sem.at[2])
    in_copy.start()
    out_copy = pltpu.make_async_copy(w_out_hbm, w_out, local_sem.at[3])
    out_copy.start()

    barrier = pltpu.get_barrier_semaphore()
    @pl.loop(0, ring - 1)
    def _(step):
        pl.semaphore_signal(barrier, inc=1, device_id=far(step), device_id_type=pl.DeviceIdType.MESH)

    for one, two in around:
        there = (z * PEERS + near_index(one), beside_index(two))
        pl.semaphore_signal(barrier, inc=1, device_id=there, device_id_type=pl.DeviceIdType.MESH)

    owner_copy.wait()
    offset_copy.wait()
    owner = owner_v[...]
    code = owner * table.shape[0] + offset_v[...]
    id_near[p] = jnp.broadcast_to(code, (8, tokens))
    id_seq[seq] = id_near[p]
    pl.semaphore_wait(barrier, len(around) + ring - 1)

    for step in range(PEERS - 1):
        send(id_near.at[p], id_near.at[p], ID_NEAR, near(step))
    leaving.append((ID_NEAR, id_near.at[pl.ds(0, PEERS - 1)]))
    for step in range(HEADS - 1):
        send(id_seq.at[seq], id_seq.at[seq], ID_SEQ, beside(step))
    leaving.append((ID_SEQ, id_seq.at[pl.ds(0, HEADS - 1)]))

    n_sub = iota((tokens, tokens), 0)
    n_lane = iota((tokens, tokens), 1)

    def both_ways(owners):
        wide = jnp.broadcast_to(owners.astype(F32), (tokens, tokens))
        return wide, wide.T

    owner_lane, owner_sub = both_ways(owner)
    second_lane = jnp.max(
        jnp.where((owner_lane == owner_sub) & (n_sub < n_lane), 1.0, 0.0), axis=0, keepdims=True
    )
    slot_lane = (owner // PEERS) * block + second_lane.astype(jnp.int32) * PEERS + owner % PEERS
    place_out = jnp.where(iota((slots, tokens), 0) == slot_lane, 1.0, 0.0).astype(BF16)

    def picker(owners):
        lane, sub = both_ways(owners)
        second = jnp.max(
            jnp.where((lane == sub) & (n_lane < n_sub), 1.0, 0.0), axis=1, keepdims=True
        ).astype(jnp.int32)
        owner_of = sub[:, :1].astype(jnp.int32)
        slot = (owner_of % PEERS) * chunk_rows + (owner_of // PEERS) * 2 + second
        return jnp.where(iota((tokens, slots), 1) == slot, 1.0, 0.0).astype(BF16)

    row_to = iota((slots, slots), 0)
    row_from = iota((slots, slots), 1)
    rest = row_to % chunk_rows
    source_row = (rest // 2) * block + (rest % 2) * PEERS + row_to // chunk_rows
    regroup = jnp.where(row_from == source_row, 1.0, 0.0).astype(BF16)

    await_bytes(id_near.at[pl.ds(0, PEERS - 1)], recv_sem.at[ID_NEAR])
    id_all[z] = jnp.concatenate([id_near[i, 0:1, :] for i in range(PEERS)], axis=0)

    @pl.loop(0, ring - 1)
    def _(step):
        send(id_all.at[z], id_all.at[z], ID_FAR, far(step))

    leaving.append((ID_FAR, id_all.at[pl.ds(0, ring - 1)]))
    up_copy.wait()
    spread_all(up_all, 0, tokens, UP)

    in_copy.wait()
    for i in range(4 * HEADS):
        columns = slice(i * head, (i + 1) * head)
        w_head[columns, :] = w_in[:, columns].T
    group = HEADS * tokens
    edge = 2 * tokens
    act[:, :edge] = jnp.zeros((4 * width, edge), BF16)
    act[:, edge + group :] = jnp.zeros((4 * width, edge), BF16)
    grad_out[:, group:] = jnp.zeros((width, edge), BF16)
    for h in range(HEADS):
        kv_rows[0, h, :edge, :] = jnp.zeros((edge, head), BF16)
        weights[h, edge:, group:] = jnp.zeros((group, edge), BF16)
        slopes[h, edge:, group:] = jnp.zeros((group, edge), F32)
        slopes[h, :edge, :group] = jnp.zeros((edge, group), F32)
    table_copy.wait()
    out_copy.wait()

    await_bytes(id_all.at[pl.ds(0, ring - 1)], recv_sem.at[ID_FAR])
    codes = id_all[...].reshape(ring * PEERS, tokens)
    wanted = (codes // table.shape[0]) == me
    offsets = (codes % table.shape[0]).astype(F32)
    place = iota((ring * PEERS, tokens), 1).astype(F32)
    first = jnp.min(jnp.where(wanted, place, 1000.0), axis=1, keepdims=True)
    last = jnp.max(jnp.where(wanted, place, -1.0), axis=1, keepdims=True)
    first_off = jnp.sum(jnp.where(place == first, offsets, 0.0), axis=1, keepdims=True)
    last_off = jnp.sum(jnp.where(place == last, offsets, 0.0), axis=1, keepdims=True)
    none = float(table.shape[0])
    first_off = jnp.where(first < 1000.0, first_off, none)
    last_off = jnp.where(last > first, last_off, none)
    row_id = iota((ring * PEERS, table.shape[0]), 1).astype(F32)

    def interleave(one, two):
        both = [x.reshape(ring, PEERS, x.shape[1]) for x in (one, two)]
        return jnp.concatenate(both, axis=1).reshape(slots, one.shape[1])

    chosen = interleave(
        jnp.where(row_id == first_off, 1.0, 0.0), jnp.where(row_id == last_off, 1.0, 0.0)
    ).astype(BF16)
    for c in range(ROW_PARTS):
        rows_out[c] = mul_nn(chosen, table[:, c * row_part : (c + 1) * row_part]).astype(BF16)
        mine = rows(z * block, block)

        @pl.loop(0, ring - 1)
        def _(step, c=c, mine=mine):
            there = rows(far_index(step) * block, block)
            send(rows_out.at[c, there, :], rows_z.at[c, mine, :], Z0 + c, far(step))

        leaving.append((Z0 + c, rows_z.at[c, pl.ds(0, slots - block), :]))

        rows_z[c, mine, :] = rows_out[c, mine, :]

    slot_off = interleave(
        jnp.broadcast_to(first_off, (ring * PEERS, tokens)),
        jnp.broadcast_to(last_off, (ring * PEERS, tokens)),
    ).T[:8]
    high = jnp.floor(slot_off * 0.0625)
    digits = jnp.concatenate([high, slot_off - 16.0 * high], axis=0).astype(BF16)
    moved = mul_nt(digits, regroup)
    slot_rows[seq] = moved[:8] * 16.0 + moved[8:]
    for step in range(HEADS - 1):
        send(slot_rows.at[seq], slot_rows.at[seq], SLOTS, beside(step))
    leaving.append((SLOTS, slot_rows.at[pl.ds(0, HEADS - 1)]))

    settle_all(up_all, 0, tokens, UP)
    grad_gated[...] = mul_nt(w_out[...], up_all[...])
    up_t[...] = up_all[rows(seq * tokens, tokens), :].astype(F32).T
    await_bytes(id_seq.at[pl.ds(0, HEADS - 1)], recv_sem.at[ID_SEQ])
    pick_in = [picker(id_seq[i, 0:1, :] // table.shape[0]) for i in range(HEADS)]

    def pass_around(c, src, src_sem, mid, dst, sem):
        await_bytes(src.at[c, pl.ds(0, slots - block), :], recv_sem.at[src_sem + c])
        mid[c] = mul_nn(regroup, src[c]).astype(BF16)
        mine = rows(seq * slots + p * chunk_rows, chunk_rows)
        for one, two in around:
            to = near_index(one)
            there = rows(to * chunk_rows, chunk_rows)
            device = (z * PEERS + to, beside_index(two))
            send(mid.at[c, there, :], dst.at[c, mine, :], sem + c, device)
        leaving.append((sem + c, dst.at[c, pl.ds(0, HEADS * slots - chunk_rows), :]))
        dst[c, mine, :] = mid[c, rows(p * chunk_rows, chunk_rows), :]

    def arrive_around(c, dst, sem):
        await_bytes(dst.at[c, pl.ds(0, HEADS * slots - chunk_rows), :], recv_sem.at[sem + c])

    for c in range(ROW_PARTS):
        pass_around(c, rows_z, Z0, rows_x, rows_in, X0)
    for c in range(ROW_PARTS):
        arrive_around(c, rows_in, X0)
        for i in range(HEADS):
            found = mul_nn(pick_in[i], rows_in[c, i * slots : (i + 1) * slots, :])
            emb_all[c, i * tokens : (i + 1) * tokens, :] = found.astype(BF16)

    own = rows(seq * tokens, tokens)
    emb_own = jnp.concatenate([emb_all[c, own, :] for c in range(ROW_PARTS)], axis=1).astype(F32)
    emb_t = emb_own.T
    centered_t = emb_t - jnp.mean(emb_t, axis=0, keepdims=True)
    inv_own = lax.rsqrt(jnp.mean(centered_t * centered_t, axis=0, keepdims=True) + EPS)
    normed_t[...] = centered_t * inv_own

    for i in range(HEADS):
        here = slice(i * tokens, (i + 1) * tokens)
        wide = jnp.concatenate([emb_all[c, here, :] for c in range(ROW_PARTS)], axis=1).astype(F32)
        centered = wide - jnp.mean(wide, axis=1, keepdims=True)
        inv = lax.rsqrt(jnp.mean(centered * centered, axis=1, keepdims=True) + EPS)
        normed_bf[here, :] = (centered * inv).astype(BF16)

    pre[...] = mul_nt(w_head[...], normed_bf[...])
    inside = slice(edge, edge + group)

    def head_of(i, h):
        return slice(i * width + h * head, i * width + (h + 1) * head)

    for i in range(4):
        for h in range(HEADS):
            x = pre[head_of(i, h), :]
            found = (x * jax.nn.sigmoid(x)).astype(BF16)
            act[head_of(i, h), inside] = found
            if i == 1:
                kv_rows[0, h, inside, :] = found.T
            if i == 3:
                kv_rows[1, h, inside, :] = found.T
    GATE, VALUE, QUERY, KEY = range(4)

    lengths_copy.wait()
    start_two = lengths[0, 0]
    start_three = start_two + lengths[0, 1]

    def user_of(position):
        return (position >= start_two).astype(jnp.int32) + (position >= start_three).astype(jnp.int32)

    scale = head ** (-0.5)
    for j in range(HEADS):
        low = max(0, j - 2) * tokens
        count = (j + 1) * tokens - low
        here = slice(j * tokens, (j + 1) * tokens)
        here_in = slice(edge + j * tokens, edge + (j + 1) * tokens)
        ms_in = slice(edge + low, edge + low + count)
        m_at = iota((count, 1), 0) + low
        n_at = iota((1, tokens), 1) + j * tokens
        allowed = (user_of(m_at) == user_of(n_at)) & (m_at <= n_at)
        for h in range(HEADS):
            scores = mul_nn(kv_rows[1, h, ms_in, :], act[head_of(QUERY, h), here_in]) * scale
            logistic = jax.nn.sigmoid(scores)
            weight = jnp.where(allowed, scores * logistic, 0.0).astype(BF16)
            weights[h, ms_in, here] = weight
            slopes[h, ms_in, here] = jnp.where(
                allowed, logistic * (1.0 + scores * (1.0 - logistic)) * scale, 0.0
            )
            attended[head_of(0, h), here] = mul_nn(act[head_of(VALUE, h), ms_in], weight)
        out = attended[:, here]
        g = grad_gated[:, here] * act[:width, here_in].astype(F32)
        out = out - jnp.mean(out, axis=0, keepdims=True)
        inv_out = lax.rsqrt(jnp.mean(out * out, axis=0, keepdims=True) + EPS)
        out = out * inv_out
        attended[:, here] = out
        slant = jnp.mean(g * out, axis=0, keepdims=True)
        grad_out[:, here] = (
            inv_out * (g - jnp.mean(g, axis=0, keepdims=True) - out * slant)
        ).astype(BF16)

    at = pl.multiple_of(seq * tokens, tokens)
    own_n = pl.ds(at, tokens)
    own_in = pl.ds(pl.multiple_of(edge + at, tokens), tokens)
    reach = pl.ds(at, 3 * tokens)
    later_in = pl.ds(pl.multiple_of(edge + at, tokens), 3 * tokens)

    def slope(part_of):
        x = pre[part_of, own_n]
        logistic = jax.nn.sigmoid(x)
        return logistic * (1.0 + x * (1.0 - logistic))

    normed_out = attended[:, own_n]
    gated[...] = (normed_out * act[:width, own_in].astype(F32)).astype(BF16)
    gate = slice(0, width)
    gp_in[gate, :] = (grad_gated[:, own_n] * normed_out * slope(gate)).astype(BF16)
    for h in range(HEADS):
        of_head = head_of(0, h)
        grad_later = grad_out[of_head, reach]
        found = mul_nt(grad_later, weights[h, own_in, reach])
        to = head_of(VALUE, h)
        gp_in[to, :] = (found * slope(to)).astype(BF16)
        score = mul_nn(kv_rows[0, h, reach, :], grad_out[of_head, own_n])
        score = (score * slopes[h, reach, own_n]).astype(BF16)
        found = mul_nn(act[head_of(KEY, h), reach], score)
        to = head_of(QUERY, h)
        gp_in[to, :] = (found * slope(to)).astype(BF16)
        score = mul_nn(kv_rows[0, h, own_in, :], grad_later)
        score = (score * slopes[h, own_in, reach]).astype(BF16)
        found = mul_nt(act[head_of(QUERY, h), later_in], score)
        to = head_of(KEY, h)
        gp_in[to, :] = (found * slope(to)).astype(BF16)

    grad_normed = mul_nn(w_in[...], gp_in[...])
    normed = normed_t[...]
    grad_rows = up_t[...] + inv_own * (
        grad_normed
        - jnp.mean(grad_normed, axis=0, keepdims=True)
        - normed * jnp.mean(grad_normed * normed, axis=0, keepdims=True)
    )
    grad_rows = grad_rows.astype(BF16)
    for c in range(GRAD_PARTS):
        g_out[c] = mul_nt(place_out, grad_rows[c * grad_part : (c + 1) * grad_part]).astype(BF16)
        mine = rows(z * block, block)

        @pl.loop(0, ring - 1)
        def _(step, c=c, mine=mine):
            there = rows(far_index(step) * block, block)
            send(g_out.at[c, there, :], g_z.at[c, mine, :], GZ0 + c, far(step))

        leaving.append((GZ0 + c, g_z.at[c, pl.ds(0, slots - block), :]))

        g_z[c, mine, :] = g_out[c, mine, :]

    layer_ref[...] = (emb_own + mul_nn(gated[...].T, w_out[...])).astype(BF16)

    await_bytes(slot_rows.at[pl.ds(0, HEADS - 1)], recv_sem.at[SLOTS])
    table_row = iota((table.shape[0], slots), 0).astype(F32)
    placed = jnp.concatenate(
        [
            jnp.where(table_row == slot_rows[i, 0:1, :], 1.0, 0.0).astype(BF16)
            for i in range(HEADS)
        ],
        axis=1,
    )

    for c in range(GRAD_PARTS):
        pass_around(c, g_z, GZ0, g_x, g_in, GX0)
    for c in range(GRAD_PARTS):
        arrive_around(c, g_in, GX0)
        grad_ref[:, c * grad_part : (c + 1) * grad_part] = mul_nn(placed, g_in[c])

    for group, view in leaving:
        await_bytes(view, send_sem.at[group])


def local(embedding_table, project_in, project_out, row_owner, row_offset, user_lengths, upstream):
    tokens = row_offset.shape[0]
    table_rows, width = embedding_table.shape
    ring = lax.axis_size("table") // PEERS
    group = tokens * HEADS
    slots = 2 * PEERS * ring
    head = width // HEADS
    vmem_spec = pl.BlockSpec(memory_space=pltpu.VMEM)
    hbm_spec = pl.BlockSpec(memory_space=pltpu.HBM)
    vmem = pltpu.VMEM
    return pl.pallas_call(
        functools.partial(kernel, ring),
        out_shape=(
            vmem((tokens, width), BF16),
            vmem((table_rows, width), F32),
        ),
        in_specs=[hbm_spec] * 7,
        out_specs=(vmem_spec, vmem_spec),
        scratch_shapes=[
            vmem((1, tokens), jnp.int32),
            vmem((1, tokens), jnp.int32),
            pltpu.SMEM((1, 3), jnp.int32),
            vmem((PEERS, 8, tokens), jnp.int32),
            vmem((HEADS, 8, tokens), jnp.int32),
            vmem((ring, PEERS, tokens), jnp.int32),
            vmem((HEADS, 8, slots), F32),
            vmem((table_rows, width), BF16),
            vmem((width, 4 * width), BF16),
            vmem((width, width), BF16),
            vmem((group, width), BF16),
            vmem((4 * width, width), BF16),
            vmem((ROW_PARTS, slots, width // ROW_PARTS), BF16),
            vmem((ROW_PARTS, slots, width // ROW_PARTS), BF16),
            vmem((ROW_PARTS, slots, width // ROW_PARTS), BF16),
            vmem((ROW_PARTS, HEADS * slots, width // ROW_PARTS), BF16),
            vmem((ROW_PARTS, group, width // ROW_PARTS), BF16),
            vmem((group, width), BF16),
            vmem((4 * width, group), F32),
            vmem((4 * width, 2 * group), BF16),
            vmem((2, HEADS, group + 2 * tokens, head), BF16),
            vmem((HEADS, group + 2 * tokens, group + 2 * tokens), BF16),
            vmem((HEADS, group + 2 * tokens, group + 2 * tokens), F32),
            vmem((width, group), F32),
            vmem((width, group), F32),
            vmem((width, group + 2 * tokens), BF16),
            vmem((width, tokens), BF16),
            vmem((4 * width, tokens), BF16),
            vmem((width, tokens), F32),
            vmem((width, tokens), F32),
            vmem((GRAD_PARTS, slots, width // GRAD_PARTS), BF16),
            vmem((GRAD_PARTS, slots, width // GRAD_PARTS), BF16),
            vmem((GRAD_PARTS, slots, width // GRAD_PARTS), BF16),
            vmem((GRAD_PARTS, HEADS * slots, width // GRAD_PARTS), BF16),
            pltpu.SemaphoreType.DMA((7,)),
            pltpu.SemaphoreType.DMA((5 + 2 * ROW_PARTS + 2 * GRAD_PARTS,)),
            pltpu.SemaphoreType.DMA((5 + 2 * ROW_PARTS + 2 * GRAD_PARTS,)),
        ],
        compiler_params=pltpu.CompilerParams(
            collective_id=0, has_side_effects=True, vmem_limit_bytes=58 * 2**20
        ),
        name="hstu_step",
    )(
        row_owner.reshape(1, tokens),
        row_offset.reshape(1, tokens),
        user_lengths,
        embedding_table,
        project_in,
        project_out,
        upstream,
    )


def solution(mesh):
    return jax.shard_map(
        local,
        mesh=mesh,
        in_specs=(
            P("table", None),
            P(),
            P(),
            P(("table", "seq"), None),
            P(("table", "seq")),
            P("table", None),
            P(("table", "seq"), None),
        ),
        out_specs=(P(("table", "seq"), None), P("table", None)),
        check_vma=False,
    )
```

time: 87.4 us -> 81.5 us (0.932)
  Pallas kernels: 85 us -> 79.1 us
    pallas_call x1, Pallas kernels: 85 us -> 79.1 us  [local(): pl.pallas_call(functools.partial(kernel, ring), out_shape=(vmem((tokens,...]
where the time goes in v4:
time: 81.5 us; the launch traced here: 81.4 us
  Pallas kernels  79.1 us (97%)
  local copies, waits for them, and re-layouts  1.63 us (2%)
    pallas_call x1, Pallas kernels, local(): pl.pallas_call(functools.partial(kernel, ring), out_shape=(vmem((tokens,...  79.1 us

profile of v4, /device:TPU:1, one launch (start us, length us, event | category | flops | bytes accessed | tf_op | source)
XLA Modules:
  0.0 81.4 jit_solution(10282631292768597579)
XLA Ops:
  0.6 79.1 %hstu_step.1 = (bf16[128,512]{1,0:T(8,128)(2,1)S(1)}, f32[512,512]{1,0:T(8,128)S(1)}) custom-call(s32[1,128]{1,0:T(1,128)} %bitcast.2, s32[1,128]{1,0:T(1,128)} %bitcast.3, s32[1,3]{1,0:T(1,128)} %lengths_hbm.1, bf16[512,512]{1,0:T(8,128)(2,1)} %table_hbm.1, bf16[512,2048]{1,0:T(8,128)(2,1)} %w_in_hbm.1, bf16[512,512]{1,0:T(8,128)(2,1)} %w_out_hbm.1, ...), custom_call_target="tpu_custom_call" | custom-call | tf_op jit(solution)/shard_map/hstu_step/pallas_call | solution.py:482
  79.7 0.7 copy.11
  80.4 1.0 %copy.12 = f32[512,512]{1,0:T(8,128)} copy(f32[512,512]{1,0:T(8,128)S(1)} %get-tuple-element.3) | data formatting | bytes 2097152

commit v5 on v4

--- a/solution.py
+++ b/solution.py
@@ -65,7 +65,6 @@
     grad_gated,
     attended,
     grad_out,
-    gated,
     gp_in,
     normed_t,
     up_t,
@@ -100,10 +99,10 @@
     def near(step):
         return (z * PEERS + near_index(step), seq)
 
-    around = [(near, beside) for beside in (2, 0, 1) for near in (4, 5, 0, 1, 2, 3, 6)]
-    around = around[:2] + around[7:9] + around[14:16] + around[2:7] + around[9:14] + around[16:]
-    around += [(near, 3) for near in range(PEERS - 1)]
-    around += [(PEERS - 1, beside) for beside in (2, 0, 1)]
+    every = [(i % PEERS, i // PEERS) for i in range(PEERS * HEADS - 1)]
+    mixed = [every[13 * i % len(every)] for i in range(len(every))]
+    hops = [(1, 1, 1, 1, 2, 2, 0, 0)[one] + (1, 1, 2, 0)[two] for one, two in mixed]
+    around = [pair for far in (4, 3, 2, 1, 0) for pair, h in zip(mixed, hops) if h == far]
 
     def turn(i):
         hops = (ring - i) // 2
@@ -406,27 +405,35 @@
         return logistic * (1.0 + x * (1.0 - logistic))
 
     normed_out = attended[:, own_n]
-    gated[...] = (normed_out * act[:width, own_in].astype(F32)).astype(BF16)
     gate = slice(0, width)
     gp_in[gate, :] = (grad_gated[:, own_n] * normed_out * slope(gate)).astype(BF16)
+
+    def part_normed(i):
+        columns = slice(i * width, (i + 1) * width)
+        return mul_nn(w_in[:, columns], gp_in[columns, :])
+
+    as_query, as_key = [], []
     for h in range(HEADS):
-        of_head = head_of(0, h)
-        grad_later = grad_out[of_head, reach]
-        found = mul_nt(grad_later, weights[h, own_in, reach])
+        score = mul_nn(kv_rows[0, h, reach, :], grad_out[head_of(0, h), own_n])
+        as_query.append((score * slopes[h, reach, own_n]).astype(BF16))
+        score = mul_nn(kv_rows[0, h, own_in, :], grad_out[head_of(0, h), reach])
+        as_key.append((score * slopes[h, own_in, reach]).astype(BF16))
+    grad_normed = part_normed(GATE)
+    for h in range(HEADS):
         to = head_of(VALUE, h)
+        found = mul_nt(grad_out[head_of(0, h), reach], weights[h, own_in, reach])
         gp_in[to, :] = (found * slope(to)).astype(BF16)
-        score = mul_nn(kv_rows[0, h, reach, :], grad_out[of_head, own_n])
-        score = (score * slopes[h, reach, own_n]).astype(BF16)
-        found = mul_nn(act[head_of(KEY, h), reach], score)
+    grad_normed = grad_normed + part_normed(VALUE)
+    for h in range(HEADS):
         to = head_of(QUERY, h)
+        found = mul_nn(act[head_of(KEY, h), reach], as_query[h])
         gp_in[to, :] = (found * slope(to)).astype(BF16)
-        score = mul_nn(kv_rows[0, h, own_in, :], grad_later)
-        score = (score * slopes[h, own_in, reach]).astype(BF16)
-        found = mul_nt(act[head_of(QUERY, h), later_in], score)
+    grad_normed = grad_normed + part_normed(QUERY)
+    for h in range(HEADS):
         to = head_of(KEY, h)
+        found = mul_nt(act[head_of(QUERY, h), later_in], as_key[h])
         gp_in[to, :] = (found * slope(to)).astype(BF16)
-
-    grad_normed = mul_nn(w_in[...], gp_in[...])
+    grad_normed = grad_normed + part_normed(KEY)
     normed = normed_t[...]
     grad_rows = up_t[...] + inv_own * (
         grad_normed
@@ -447,7 +454,8 @@
 
         g_z[c, mine, :] = g_out[c, mine, :]
 
-    layer_ref[...] = (emb_own + mul_nn(gated[...].T, w_out[...])).astype(BF16)
+    gated = (attended[:, own_n] * act[:width, own_in].astype(F32)).astype(BF16)
+    layer_ref[...] = (emb_own + mul_nn(gated.T, w_out[...])).astype(BF16)
 
     await_bytes(slot_rows.at[pl.ds(0, HEADS - 1)], recv_sem.at[SLOTS])
     table_row = iota((table.shape[0], slots), 0).astype(F32)
@@ -514,7 +522,6 @@
             vmem((width, group), F32),
             vmem((width, group), F32),
             vmem((width, group + 2 * tokens), BF16),
-            vmem((width, tokens), BF16),
             vmem((4 * width, tokens), BF16),
             vmem((width, tokens), F32),
             vmem((width, tokens), F32),

time: 81.5 us -> 80 us (0.982)
  Pallas kernels: 79.1 us -> 77.7 us
    pallas_call x1, Pallas kernels: 79.1 us -> 77.7 us  [local(): pl.pallas_call(functools.partial(kernel, ring), out_shape=(vmem((tokens,...]
where the time goes in v5:
time: 80 us; the launch traced here: 79.9 us
  Pallas kernels  77.7 us (97%)
  local copies, waits for them, and re-layouts  1.63 us (2%)
    pallas_call x1, Pallas kernels, local(): pl.pallas_call(functools.partial(kernel, ring), out_shape=(vmem((tokens,...  77.7 us
    unnamed x2, local copies, waits for them, and re-layouts  1.63 us

profile of v5, /device:TPU:1, one launch (start us, length us, event | category | flops | bytes accessed | tf_op | source)
XLA Modules:
  0.0 79.9 jit_solution(12729215471521517198)
XLA Ops:
  0.6 77.7 %hstu_step.1 = (bf16[128,512]{1,0:T(8,128)(2,1)S(1)}, f32[512,512]{1,0:T(8,128)S(1)}) custom-call(s32[1,128]{1,0:T(1,128)} %bitcast.2, s32[1,128]{1,0:T(1,128)} %bitcast.3, s32[1,3]{1,0:T(1,128)} %lengths_hbm.1, bf16[512,512]{1,0:T(8,128)(2,1)} %table_hbm.1, bf16[512,2048]{1,0:T(8,128)(2,1)} %w_in_hbm.1, bf16[512,512]{1,0:T(8,128)(2,1)} %w_out_hbm.1, ...), custom_call_target="tpu_custom_call" | custom-call | tf_op jit(solution)/shard_map/hstu_step/pallas_call | solution.py:490
  78.3 0.7 copy.11
  79.0 1.0 %copy.12 = f32[512,512]{1,0:T(8,128)} copy(f32[512,512]{1,0:T(8,128)S(1)} %get-tuple-element.3) | data formatting | bytes 2097152
